TPU v7x, 512 devices: a whole 4x8x8 slice. The times are simulated.
512 devices in a mesh: dp: 32 (over x, y), fsdp: 16 (over z, core).
Axes of the slice: x: 4, y: 8, z: 8, core: 2. Of those that a mesh axis runs over, the one named last changes fastest.
Arguments:
- grad_parts: float32 [32, 16, 16, 28672], P('dp', 'fsdp'), may hold values from -6 to 6
- momentum: float32 [32, 16, 28672], P('dp', 'fsdp'), may hold values from -24 to 24
- positions: int32 [32, 16, 4, 448], P(None, 'fsdp'), may hold values from 0 to 63, as said below
Outputs:
- update: float32 [16, 28672], P('fsdp')
- new_momentum: float32 [32, 16, 28672], P('dp', 'fsdp')
Inputs may be any that keep to these rules, and one draw needn't show every extreme that they name: For every replica, row and block the 4 positions are different.
All inputs are finite; a program needn't handle non-finite values.
Results may differ from a plain program's by a relative error of at most 0.0003.
Values sent between devices are 32-bit elements; how exact they have to be, the bound alone decides.
No kernel may reach another device: no remote copies, remote signals or barrier semaphores. Data moves between devices by JAX's collectives and lax.ppermute only.
A program may use at most 64 MiB of HBM per device.

v0:
```python
import jax
import jax.numpy as jnp
from jax import lax
from jax.sharding import PartitionSpec as P

decay_rate = 0.999
epsilon = 1e-06


def paired_table():
    levels = jnp.arange(64, dtype=jnp.float32)
    frequency = levels[:, None]
    sample = levels[None, :]
    cosines = jnp.cos(jnp.pi * (2.0 * sample + 1.0) * frequency / 128.0)
    norming = jnp.where(frequency == 0.0, jnp.sqrt(1.0 / 64.0), jnp.sqrt(2.0 / 64.0))
    return jnp.kron(jnp.eye(2, dtype=jnp.float32), cosines * norming)


def forward(fields, paired):
    blocks = fields.reshape(fields.shape[:-1] + (fields.shape[-1] // 128, 128))
    return jnp.einsum("...n,kn->...k", blocks, paired, precision=lax.Precision.HIGHEST)


def inverse(coeffs, paired):
    fields = jnp.einsum("...k,kn->...n", coeffs, paired, precision=lax.Precision.HIGHEST)
    return fields.reshape(fields.shape[:-2] + (fields.shape[-2] * 128,))


def lookup(places):
    span_count = places.shape[-1]
    shifted = places + 64 * (jnp.arange(span_count, dtype=jnp.int32) % 2)
    grouped = shifted.reshape(places.shape[:-1] + (span_count // 2, 2))
    return grouped[..., None] == jnp.arange(128, dtype=jnp.int32)


def expand(values, places):
    hit_table = lookup(places)
    spread = values.reshape(values.shape[:-1] + (values.shape[-1] // 2, 2))[..., None]
    return jnp.sum(jnp.where(hit_table, spread, 0.0), axis=(-4, -2))


def extract(coeffs, places):
    hit_table = lookup(places)
    picked = jnp.sum(jnp.where(hit_table, coeffs[..., None, :, None, :], 0.0), axis=-1)
    return picked.reshape(places.shape)


def body(grad_parts, momentum, positions):
    paired = paired_table()
    local_rows = momentum.shape[1]
    partial_value = grad_parts[0, 0]
    own_places = lax.dynamic_index_in_dim(positions, lax.axis_index("dp"), 0, keepdims=False)
    old_moment = momentum[0]
    gradient = lax.psum_scatter(partial_value, "fsdp", scatter_dimension=0, tiled=True)
    accumulated = decay_rate * old_moment + gradient
    coeffs = forward(accumulated, paired)
    kept_values = extract(coeffs, own_places)
    own_dense = expand(kept_values, own_places)
    new_moment = accumulated - inverse(own_dense, paired)
    replicas = lax.axis_size("dp")
    initial = jnp.zeros(old_moment.shape, jnp.float32)
    shard_piece = lax.all_gather(kept_values[None], "dp", axis=0, tiled=True)

    def one_replica(step_index, inner):
        values = lax.dynamic_index_in_dim(shard_piece, step_index, 0, keepdims=False)
        places = lax.dynamic_index_in_dim(positions, step_index, 0, keepdims=False)
        return inner + inverse(expand(values, places), paired)

    gathered = lax.fori_loop(0, shard_piece.shape[0], one_replica, initial)
    averaged = gathered / replicas
    spanned = averaged.reshape(local_rows, averaged.shape[-1] // 64, 64)
    meansq = jnp.mean(spanned * spanned, axis=-1, keepdims=True)
    update = spanned / jnp.sqrt(spanned * spanned + meansq + epsilon)
    return (update.reshape(local_rows, averaged.shape[-1]), new_moment[None])


def solution(mesh):
    in_specs = (P("dp", "fsdp", None, None), P("dp", "fsdp", None), P(None, "fsdp", None, None))
    out_specs = (P("fsdp", None), P("dp", "fsdp", None))
    return jax.shard_map(body, mesh=mesh, in_specs=in_specs, out_specs=out_specs, check_vma=False)
```

profile of v0, /device:TPU:16, one launch (start us, length us, event | category | flops | bytes accessed | tf_op | source)
XLA Modules:
  0.0 294.5 jit_solution(13463209886421082663)
XLA Ops:
  8.0 0.7 constant_dynamic-slice_fusion.2
  9.6 1.3 dynamic-slice
  10.9 124.2 %all-reduce.3.cloned.1.call-done = f32[16,28672]{1,0:T(8,128)} async-done(((f32[16,28672]{1,0:T(8,128)}), f32[16,28672]{1,0:T(8,128)}) %all-reduce.3.cloned.1.call-update) | async-done | bytes 1835024
  135.2 2.0 dynamic-slice_add_fusion
  139.0 49.5 %all_gather.3 = f32[32,1,4,448]{3,2,1,0:T(4,128)S(1)} all-gather(f32[1,1,4,448]{3,2,1,0:T(4,128)S(1)} %copy.24), channel_id=1, replica_groups=mesh['dp'=32,'fsdp'=16] {'dp'}, dimensions={0}, use_global_device_ids=true | all-gather | bytes 236544 | tf_op jit(solution)/shard_map/all_gather | solution.py:62
  188.5 96.5 %while.16 = (s32[]{:T(128)}, f32[1,28672]{1,0:T(1,128)S(1)}, s32[32,1,4,448]{3,2,1,0:T(4,128)}, f32[32,1,4,448]{3,2,1,0:T(4,128)S(1)}, f32[64,64]{1,0:T(8,128)S(...) while((s32[]{:T(128)}, f32[1,28672]{1,0:T(1,128)S(1)}, s32[32,1,4,448]{3,2,1,0:T(4,128)}, ...), condition=%wide.region_4.5_spmd.clone, body=%wide.region_2.4_spmd.clone.sunk | while | flops 44781440 | bytes 1085047 | solution.py:69
  191.5 0.7 constant_dynamic-slice_fusion.6
  194.5 0.7 constant_dynamic-slice_fusion.6
  197.5 0.7 constant_dynamic-slice_fusion.6
  200.5 0.7 constant_dynamic-slice_fusion.6
  203.5 0.7 constant_dynamic-slice_fusion.6
  206.5 0.7 constant_dynamic-slice_fusion.6
  209.6 0.7 constant_dynamic-slice_fusion.6
  212.6 0.7 constant_dynamic-slice_fusion.6
  215.6 0.7 constant_dynamic-slice_fusion.6
  218.6 0.7 constant_dynamic-slice_fusion.6
  221.6 0.7 constant_dynamic-slice_fusion.6
  224.6 0.7 constant_dynamic-slice_fusion.6
  227.7 0.7 constant_dynamic-slice_fusion.6
  230.7 0.7 constant_dynamic-slice_fusion.6
  233.7 0.7 constant_dynamic-slice_fusion.6
  236.7 0.7 constant_dynamic-slice_fusion.6
  239.7 0.7 constant_dynamic-slice_fusion.6
  242.7 0.7 constant_dynamic-slice_fusion.6
  248.8 0.7 constant_dynamic-slice_fusion.6
  251.8 0.7 constant_dynamic-slice_fusion.6
  254.8 0.7 constant_dynamic-slice_fusion.6
  257.8 0.7 constant_dynamic-slice_fusion.6
  260.8 0.7 constant_dynamic-slice_fusion.6
  263.8 0.7 constant_dynamic-slice_fusion.6
  285.8 0.8 rsqrt_multiply_fusion
  286.9 0.8 subtract_bitcast_fusion
  (418 shorter events, 82.2 us)
Async XLA Ops:
  7.2 128.0 %copy-start = (f32[1,1,28672]{2,1,0:T(1,128)S(1)}, f32[1,1,28672]{2,1,0:T(1,128)}, u32[]{:S(2)}) copy-start(f32[1,1,28672]{2,1,0:T(1,128)} %param.6) | copy-start | bytes 344068
  7.2 128.0 %all-reduce.3.cloned.1.call-start = ((), (), s32[]{:S(2)}) async-start(), calls=%async_computation | async-start | bytes 3670016
Sparse Core Ops, SparseCore 0:
  10.4 124.7 all-reduce.2
where the time goes:
time: 297 us; the launch traced here: 295 us
  waiting for transfers between devices  125 us (42%)
  blocking collectives  49.5 us (17%)
  other arithmetic  48.9 us (16%)
  local copies, waits for them, and re-layouts  46.6 us (16%)
  between operations  14.2 us (5%)
  matrix products  8.37 us (3%)
    unnamed x2, waiting for transfers between devices  125 us
    all_gather x1, blocking collectives, body(): shard_piece = lax.all_gather(kept_values[None], 'dp', axis=0, tiled=True)  49.5 us
    dynamic_slice x64, local copies, waits for them, and re-layouts, one_replica(): places = lax.dynamic_index_in_dim(positions, step_index, 0, keepdims=False)  26.9 us
    reduce_sum x33, other arithmetic, expand(): return jnp.sum(jnp.where(hit_table, spread, 0.0), axis=(-4, -2))  21.2 us
    add x33, other arithmetic, lookup(): shifted = places + 64 * (jnp.arange(span_count, dtype=jnp.int32) % 2)  9.94 us
    dot_general x33, matrix products, inverse(): jnp.einsum('...k,kn->...n', coeffs, paired, precision=lax.Precision.HIGHEST)  8.11 us
    add x32, other arithmetic, one_replica(): return inner + inverse(expand(values, places), paired)  7.36 us
  transfers between devices with their start and end apart: 1, of which 1 were waited for; matrix products, arithmetic and copies ran while one was open for 1% of the time, Pallas kernels for 0%

commit v1 on v0

v1 whole, which is shorter than its diff:
```python
import functools

import jax
import jax.numpy as jnp
import numpy as np
from jax import lax
from jax.experimental import pallas as pl
from jax.experimental.pallas import tpu as pltpu
from jax.sharding import PartitionSpec as P

decay_rate = 0.999
epsilon = 1e-06
block = 64
lanes = 128
keep = 4
f32, bf16 = jnp.float32, jnp.bfloat16


def paired_table():
    frequency = np.arange(block)[:, None]
    sample = np.arange(block)[None, :]
    cosines = np.cos(np.pi * (2.0 * sample + 1.0) * frequency / (2.0 * block))
    norming = np.where(frequency == 0, np.sqrt(1.0 / block), np.sqrt(2.0 / block))
    return np.kron(np.eye(2), cosines * norming).astype(np.float32)


def split_table():
    table = paired_table()
    high = table.astype(jnp.bfloat16)
    low = (table - high.astype(np.float32)).astype(jnp.bfloat16)
    return np.stack([high, low])


def halves(x):
    high = x.astype(bf16)
    return high, (x - high.astype(f32)).astype(bf16)


def dot3(x, table_ref, dims, table_first):
    high, low = halves(x)

    def one(part, index):
        pair = (table_ref[index], part) if table_first else (part, table_ref[index])
        return lax.dot_general(*pair, (dims, ((), ())), preferred_element_type=f32)

    return one(high, 0) + (one(low, 0) + one(high, 1))


def forward(fields, table_ref):
    return dot3(fields, table_ref, ((1,), (1,)), True)


def inverse(coeffs, table_ref):
    return dot3(coeffs, table_ref, ((0,), (0,)), False)


def same_core_rows(x, odd):
    upper, lower = x[:8], x[8:]
    row = lax.broadcasted_iota(jnp.int32, upper.shape, 0)
    even_place = row % 2 == 0
    return jnp.where(
        odd,
        jnp.where(even_place, pltpu.roll(upper, 7, 0), lower),
        jnp.where(even_place, upper, pltpu.roll(lower, 1, 0)),
    )


def pack_kernel(other, odd_ref, grad_ref, out_ref, mixed):
    tiles = out_ref.shape[1]
    odd = (odd_ref[0] != 0) != other
    for tile in range(tiles):
        mixed[8 * tile : 8 * tile + 8, :] = same_core_rows(
            grad_ref[:, tile * lanes : (tile + 1) * lanes], odd
        )
    for place in range(8):
        out_ref[place // 2 + 4 * (place % 2)] = mixed[pl.ds(place, tiles, stride=8), :]


def pack(grad, odd, other):
    rows, columns = grad.shape
    tiles = columns // lanes
    steps = 4
    step_tiles = tiles // steps
    return pl.pallas_call(
        functools.partial(pack_kernel, other),
        grid=(steps,),
        in_specs=[
            pl.BlockSpec(memory_space=pltpu.SMEM),
            pl.BlockSpec((rows, step_tiles * lanes), lambda i: (0, i)),
        ],
        out_specs=pl.BlockSpec((rows // 2, step_tiles, lanes), lambda i: (0, i, 0)),
        out_shape=jax.ShapeDtypeStruct((rows // 2, tiles, lanes), f32),
        scratch_shapes=[pltpu.VMEM((8 * step_tiles, lanes), f32)],
        cost_estimate=pl.CostEstimate(flops=rows * columns, bytes_accessed=6 * rows * columns, transcendentals=0),
        name="pack_other" if other else "pack_own",
    )(odd, grad)


def places_kernel(places_ref, out_ref):
    replicas, count, spans = places_ref.shape
    half = spans // 2
    source = lax.broadcasted_iota(jnp.int32, (spans, half), 0)
    target = lax.broadcasted_iota(jnp.int32, (spans, half), 1)
    places = places_ref[...].reshape(replicas * count, spans).astype(f32).astype(bf16)
    for parity in range(2):
        chooser = (source == 2 * target + parity).astype(f32).astype(bf16)
        chosen = jnp.dot(places, chooser, preferred_element_type=f32)
        out_ref[:, parity * count : (parity + 1) * count, :] = chosen.reshape(replicas, count, half)


def split_places(positions):
    replicas, count, spans = positions.shape
    return pl.pallas_call(
        places_kernel,
        out_shape=jax.ShapeDtypeStruct((replicas, 2 * count, spans // 2), f32),
        cost_estimate=pl.CostEstimate(flops=2 * replicas * count * spans * spans, bytes_accessed=8 * replicas * count * spans, transcendentals=0),
        name="split_places",
    )(positions)


def moment_kernel(me_ref, parts_ref, moment_ref, places_ref, table_ref, kept_ref, new_ref):
    accumulated = decay_rate * moment_ref[...]
    gradient = parts_ref[0]
    for source in range(1, parts_ref.shape[0]):
        gradient = gradient + parts_ref[source]
    accumulated = accumulated + gradient
    coeffs = forward(accumulated, table_ref)
    half = coeffs.shape[1]
    level = lax.broadcasted_iota(jnp.int32, (block, half), 0).astype(f32)
    own = places_ref[me_ref[0]]
    dense = []
    for parity in range(2):
        mine = coeffs[parity * block : (parity + 1) * block]
        inside = jnp.zeros_like(mine)
        for j in range(keep):
            row = parity * keep + j
            picked = jnp.where(own[row : row + 1] == level, mine, 0.0)
            inside = inside + picked
            kept_ref[row : row + 1, :] = jnp.sum(picked, axis=0, keepdims=True)
        dense.append(inside)
    new_ref[...] = accumulated - inverse(jnp.concatenate(dense, axis=0), table_ref)


def moment_step(me, parts, moment, places, table):
    sources, tiles, width = parts.shape
    whole = pl.BlockSpec(memory_space=pltpu.VMEM)
    return pl.pallas_call(
        moment_kernel,
        in_specs=[pl.BlockSpec(memory_space=pltpu.SMEM), whole, whole, whole, whole],
        out_specs=[whole, whole],
        out_shape=[
            jax.ShapeDtypeStruct((2 * keep, tiles), f32),
            jax.ShapeDtypeStruct((tiles, width), f32),
        ],
        cost_estimate=pl.CostEstimate(flops=12 * tiles * width * width, bytes_accessed=4 * (sources + 2) * tiles * width, transcendentals=0),
        name="moment_step",
    )(me, parts, moment, places, table)


def update_kernel(kept_ref, places_ref, table_ref, out_ref):
    replicas, _, half = kept_ref.shape
    level = lax.broadcasted_iota(jnp.int32, (block, half), 0).astype(f32)

    def one_replica(r, sums):
        values, places = kept_ref[r], places_ref[r]
        added = []
        for parity in range(2):
            dense = jnp.zeros((block, half), f32)
            for j in range(keep):
                row = parity * keep + j
                dense = jnp.where(places[row : row + 1] == level, values[row : row + 1], dense)
            added.append(sums[parity] + dense)
        return tuple(added)

    empty = jnp.zeros((block, half), f32)
    sums = lax.fori_loop(0, replicas, one_replica, (empty, empty), unroll=2)
    averaged = inverse(jnp.concatenate(sums, axis=0), table_ref) * (1.0 / replicas)
    squares = averaged * averaged
    high, low = halves(squares)
    row = lax.broadcasted_iota(jnp.int32, (lanes, lanes), 0) // block
    column = lax.broadcasted_iota(jnp.int32, (lanes, lanes), 1) // block
    same = (row == column).astype(f32).astype(bf16)
    meansq = jnp.dot(high, same, preferred_element_type=f32) + jnp.dot(low, same, preferred_element_type=f32)
    out_ref[...] = averaged * lax.rsqrt(squares + meansq * (1.0 / block) + epsilon)


def update_step(kept, places, table):
    replicas, _, half = kept.shape
    return pl.pallas_call(
        update_kernel,
        out_shape=jax.ShapeDtypeStruct((half, lanes), f32),
        cost_estimate=pl.CostEstimate(flops=9 * replicas * lanes * half, bytes_accessed=8 * kept.size, transcendentals=lanes * half),
        name="update_step",
    )(kept, places, table)


def body(grad_parts, momentum, positions):
    columns = momentum.shape[-1]
    tiles = columns // lanes
    devices = lax.axis_size("fsdp")
    replicas = lax.axis_size("dp")
    me = lax.axis_index("fsdp")
    odd = (me % 2).reshape(1)
    grad = grad_parts[0, 0]
    table = jnp.asarray(split_table())
    sent = pack(grad, odd, True)
    arrived = lax.ppermute(sent, "fsdp", [(i, i ^ 1) for i in range(devices)])
    own = pack(grad, odd, False)
    places = split_places(positions[:, 0])
    groups = [list(range(core, devices, 2)) for core in range(2)]
    parts = lax.all_to_all(own + arrived, "fsdp", 0, 0, tiled=True, axis_index_groups=groups)
    kept, new_moment = moment_step(
        lax.axis_index("dp").reshape(1), parts, momentum.reshape(tiles, lanes), places, table
    )
    everyone = lax.all_to_all(
        jnp.broadcast_to(kept[None], (replicas,) + kept.shape), "dp", 0, 0, tiled=True
    )
    update = update_step(everyone, places, table)
    return update.reshape(1, columns), new_moment.reshape(1, 1, columns)


def solution(mesh):
    in_specs = (P("dp", "fsdp", None, None), P("dp", "fsdp", None), P(None, "fsdp", None, None))
    out_specs = (P("fsdp", None), P("dp", "fsdp", None))
    return jax.shard_map(body, mesh=mesh, in_specs=in_specs, out_specs=out_specs, check_vma=False)
```

time: 297 us -> 79.7 us (0.27)
  the two profiles are of different devices: /device:TPU:16 before, /device:TPU:8 now
where the time goes in v1:
time: 79.7 us; the launch traced here: 79.2 us
  waiting for transfers between devices  24.7 us (31%)
  blocking collectives  22.6 us (28%)
  Pallas kernels  15.2 us (19%)
  starting transfers between devices  12.2 us (15%)
  other arithmetic  2.2 us (3%)
  local copies, waits for them, and re-layouts  1.64 us (2%)
    all_to_all x1, waiting for transfers between devices, body(): lax.all_to_all(own + arrived, 'fsdp', 0, 0, tiled=True, axis_index_groups...  24.7 us
    all_to_all x1, blocking collectives, body(): lax.all_to_all(jnp.broadcast_to(kept[None], (replicas,) + kept.shape), 'd...  22.6 us
    all_to_all x1, starting transfers between devices, body(): lax.all_to_all(own + arrived, 'fsdp', 0, 0, tiled=True, axis_index_groups...  10.3 us
    pallas_call x2, Pallas kernels, pack(): pl.pallas_call(functools.partial(pack_kernel, other), grid=(steps,), in_s...  7.3 us
    pallas_call x1, Pallas kernels, update_step(): pl.pallas_call(update_kernel, out_shape=jax.ShapeDtypeStruct((half, lanes...  3.48 us
    pallas_call x1, Pallas kernels, moment_step(): pl.pallas_call(moment_kernel, in_specs=[pl.BlockSpec(memory_space=pltpu.S...  2.53 us
    add x1, other arithmetic, body(): own + arrived  2.2 us
    ppermute x1, starting transfers between devices, body(): arrived = lax.ppermute(sent, 'fsdp', [(i, i ^ 1) for i in range(devices)])  1.91 us
  transfers between devices with their start and end apart: 2, of which 1 were waited for; matrix products, arithmetic and copies ran while one was open for 0% of the time, Pallas kernels for 7%

profile of v1, /device:TPU:8, one launch (start us, length us, event | category | flops | bytes accessed | tf_op | source)
XLA Modules:
  0.0 79.2 jit_solution(1684021073599772560)
XLA Ops:
  0.6 3.6 %pack_other.1 = f32[8,224,128]{2,1,0:T(8,128)} custom-call(s32[1]{0:T(128)} %bitcast.1.odd_ref, f32[16,28672]{1,0:T(8,128)} %bitcast.7), custom_call_target="tpu_custom_call" | custom-call | flops 458752 | bytes 2752512 | tf_op jit(solution)/shard_map/pack_other/pallas_call | solution.py:84
  4.3 1.9 %collective-permute-start = (f32[8,224,128]{2,1,0:T(8,128)}, f32[8,224,128]{2,1,0:T(8,128)S(1)}, u32[]{:S(2)}, u32[]{:S(2)}) collective-permute-start(f32[8,224,128]{2,1,0:T(8,128)} %pack_other.1), channel_id=1, source_target_pairs={{0,1},{1,0},{2,3},{3,2},{4,5},{5,4},{6,7},{7,6},{8,9},{9,8},{10,11... | collective-permute-start | bytes 2752520 | tf_op jit(solution)/shard_map/ppermute | solution.py:207
  6.2 3.7 %pack_own.1 = f32[8,224,128]{2,1,0:T(8,128)} custom-call(s32[1]{0:T(128)} %bitcast.1.odd_ref, f32[16,28672]{1,0:T(8,128)} %bitcast.8), custom_call_target="tpu_custom_call" | custom-call | flops 458752 | bytes 2752512 | tf_op jit(solution)/shard_map/pack_own/pallas_call | solution.py:84
  9.9 0.0 collective-permute-done
  9.9 2.2 %add.8 = f32[8,224,128]{2,1,0:T(8,128)} add(f32[8,224,128]{2,1,0:T(8,128)} %pack_own.1, f32[8,224,128]{2,1,0:T(8,128)S(1)} %collective-permute-done) | non-fusion elementwise | flops 229376 | bytes 2752512 | tf_op jit(solution)/shard_map/add | solution.py:211
  12.1 10.3 %all-to-all-start = ((f32[8,224,128]{2,1,0:T(8,128)}), f32[8,224,128]{2,1,0:T(8,128)S(1)}, u32[]{:S(2)}, u32[]{:S(2)}) async-start(f32[8,224,128]{2,1,0:T(8,128)} %add.8), calls=%async_computation | async-start | bytes 1835008 | tf_op jit(solution)/shard_map/all_to_all | solution.py:211
  22.4 1.9 %split_places.1.places_ref = f32[32,8,224]{2,1,0:T(8,128)} custom-call(s32[32,4,448]{2,1,0:T(4,128)} %bitcast.9), custom_call_target="tpu_custom_call" | custom-call | flops 51380224 | bytes 458752 | tf_op jit(solution)/shard_map/split_places/pallas_call | solution.py:113
  24.3 24.7 %all-to-all-done.parts_ref = f32[8,224,128]{2,1,0:T(8,128)S(1)} async-done(((f32[8,224,128]{2,1,0:T(8,128)}), f32[8,224,128]{2,1,0:T(8,128)S(1)}, u32[]{:S(2)}, u32[]{:S(2)}) %all-to-all-start) | async-done | bytes 917536 | tf_op jit(solution)/shard_map/all_to_all | solution.py:211
  49.0 0.0 copy-start
  49.0 0.9 %copy-done = f32[8,224,128]{2,1,0:T(8,128)} copy-done((f32[8,224,128]{2,1,0:T(8,128)}, f32[8,224,128]{2,1,0:T(8,128)S(1)}, u32[]{:S(2)}) %copy-start) | copy-done | bytes 917528
  49.9 2.5 %moment_step.1 = (f32[8,224]{1,0:T(8,128)}, f32[224,128]{1,0:T(8,128)}) custom-call(s32[1]{0:T(128)} %bitcast.me_ref, f32[8,224,128]{2,1,0:T(8,128)} %copy-done, f32[224,128]{1,0:T(8,128)} %bitcast.10, f32[32,8,224]{2,1,0:T(8,128)} %split_places.1.places_ref, bf16[2,128,128]{2,1,0:T(8,128)(2,1)} %constant.24.clone.table_ref), custom_call_target="tpu_custom_call" | custom-call | flops 44040192 | bytes 1146880 | tf_op jit(solution)/shard_map/moment_step/pallas_call | solution.py:147
  52.4 0.7 broadcast_in_dim.2
  53.1 22.6 %all_to_all.10.kept_ref = f32[32,8,224]{2,1,0:T(8,128)} all-to-all(f32[32,8,224]{2,1,0:T(8,128)S(1)} %broadcast_in_dim.2), channel_id=1, replica_groups=mesh['dp'=32,'fsdp'=16] {'dp'}, dimensions={0} | all-to-all | bytes 458752 | tf_op jit(solution)/shard_map/all_to_all | solution.py:215
  75.7 3.5 %update_step.1 = f32[224,128]{1,0:T(8,128)} custom-call(f32[32,8,224]{2,1,0:T(8,128)} %all_to_all.10.kept_ref, f32[32,8,224]{2,1,0:T(8,128)} %split_places.1.places_ref, bf16[2,128,128]{2,1,0:T(8,128)(2,1)} %constant.24.clone.table_ref), custom_call_target="tpu_custom_call" | custom-call | flops 8257536 | bytes 458752 | tf_op jit(solution)/shard_map/update_step/pallas_call | solution.py:189
Async XLA Ops:
  4.3 5.6 %collective-permute-start = (f32[8,224,128]{2,1,0:T(8,128)}, f32[8,224,128]{2,1,0:T(8,128)S(1)}, u32[]{:S(2)}, u32[]{:S(2)}) collective-permute-start(f32[8,224,128]{2,1,0:T(8,128)} %pack_other.1), channel_id=1, source_target_pairs={{0,1},{1,0},{2,3},{3,2},{4,5},{5,4},{6,7},{7,6},{8,9},{9,8},{10,11... | collective-permute-start | bytes 2752520 | tf_op jit(solution)/shard_map/ppermute | solution.py:207
  12.1 36.9 %all-to-all-start = ((f32[8,224,128]{2,1,0:T(8,128)}), f32[8,224,128]{2,1,0:T(8,128)S(1)}, u32[]{:S(2)}, u32[]{:S(2)}) async-start(f32[8,224,128]{2,1,0:T(8,128)} %add.8), calls=%async_computation | async-start | bytes 1835008 | tf_op jit(solution)/shard_map/all_to_all | solution.py:211
  49.0 0.9 %copy-start = (f32[8,224,128]{2,1,0:T(8,128)}, f32[8,224,128]{2,1,0:T(8,128)S(1)}, u32[]{:S(2)}) copy-start(f32[8,224,128]{2,1,0:T(8,128)S(1)} %all-to-all-done.parts_ref) | copy-start | bytes 2752516

commit v2 on v1

--- a/solution.py
+++ b/solution.py
@@ -14,6 +14,8 @@
 lanes = 128
 keep = 4
 f32, bf16 = jnp.float32, jnp.bfloat16
+whole = pl.BlockSpec(memory_space=pltpu.VMEM)
+params = pltpu.CompilerParams(vmem_limit_bytes=12 * 2**20)
 
 
 def paired_table():
@@ -65,32 +67,28 @@
     )
 
 
-def pack_kernel(other, odd_ref, grad_ref, out_ref, mixed):
-    tiles = out_ref.shape[1]
+def pack_kernel(other, odd_ref, grad_ref, out_ref):
     odd = (odd_ref[0] != 0) != other
-    for tile in range(tiles):
-        mixed[8 * tile : 8 * tile + 8, :] = same_core_rows(
-            grad_ref[:, tile * lanes : (tile + 1) * lanes], odd
+    for first in range(0, out_ref.shape[1], 8):
+        mixed = jnp.stack(
+            [
+                same_core_rows(grad_ref[:, tile * lanes : (tile + 1) * lanes], odd)
+                for tile in range(first, first + 8)
+            ]
         )
-    for place in range(8):
-        out_ref[place // 2 + 4 * (place % 2)] = mixed[pl.ds(place, tiles, stride=8), :]
+        rows = jnp.swapaxes(mixed, 0, 1)
+        for place in range(8):
+            out_ref[place // 2 + 4 * (place % 2), first : first + 8, :] = rows[place]
 
 
 def pack(grad, odd, other):
     rows, columns = grad.shape
-    tiles = columns // lanes
-    steps = 4
-    step_tiles = tiles // steps
     return pl.pallas_call(
         functools.partial(pack_kernel, other),
-        grid=(steps,),
-        in_specs=[
-            pl.BlockSpec(memory_space=pltpu.SMEM),
-            pl.BlockSpec((rows, step_tiles * lanes), lambda i: (0, i)),
-        ],
-        out_specs=pl.BlockSpec((rows // 2, step_tiles, lanes), lambda i: (0, i, 0)),
-        out_shape=jax.ShapeDtypeStruct((rows // 2, tiles, lanes), f32),
-        scratch_shapes=[pltpu.VMEM((8 * step_tiles, lanes), f32)],
+        in_specs=[pl.BlockSpec(memory_space=pltpu.SMEM), whole],
+        out_specs=whole,
+        out_shape=jax.ShapeDtypeStruct((rows // 2, columns // lanes, lanes), f32),
+        compiler_params=params,
         cost_estimate=pl.CostEstimate(flops=rows * columns, bytes_accessed=6 * rows * columns, transcendentals=0),
         name="pack_other" if other else "pack_own",
     )(odd, grad)
@@ -113,6 +111,9 @@
     return pl.pallas_call(
         places_kernel,
         out_shape=jax.ShapeDtypeStruct((replicas, 2 * count, spans // 2), f32),
+        in_specs=[whole],
+        out_specs=whole,
+        compiler_params=params,
         cost_estimate=pl.CostEstimate(flops=2 * replicas * count * spans * spans, bytes_accessed=8 * replicas * count * spans, transcendentals=0),
         name="split_places",
     )(positions)
@@ -128,7 +129,7 @@
     half = coeffs.shape[1]
     level = lax.broadcasted_iota(jnp.int32, (block, half), 0).astype(f32)
     own = places_ref[me_ref[0]]
-    dense = []
+    dense, kept = [], []
     for parity in range(2):
         mine = coeffs[parity * block : (parity + 1) * block]
         inside = jnp.zeros_like(mine)
@@ -136,22 +137,24 @@
             row = parity * keep + j
             picked = jnp.where(own[row : row + 1] == level, mine, 0.0)
             inside = inside + picked
-            kept_ref[row : row + 1, :] = jnp.sum(picked, axis=0, keepdims=True)
+            kept.append(jnp.sum(picked, axis=0, keepdims=True))
         dense.append(inside)
+    kept_ref[...] = jnp.broadcast_to(jnp.concatenate(kept, axis=0)[None], kept_ref.shape)
     new_ref[...] = accumulated - inverse(jnp.concatenate(dense, axis=0), table_ref)
 
 
 def moment_step(me, parts, moment, places, table):
+    replicas = places.shape[0]
     sources, tiles, width = parts.shape
-    whole = pl.BlockSpec(memory_space=pltpu.VMEM)
     return pl.pallas_call(
         moment_kernel,
         in_specs=[pl.BlockSpec(memory_space=pltpu.SMEM), whole, whole, whole, whole],
         out_specs=[whole, whole],
         out_shape=[
-            jax.ShapeDtypeStruct((2 * keep, tiles), f32),
+            jax.ShapeDtypeStruct((replicas, 2 * keep, tiles), f32),
             jax.ShapeDtypeStruct((tiles, width), f32),
         ],
+        compiler_params=params,
         cost_estimate=pl.CostEstimate(flops=12 * tiles * width * width, bytes_accessed=4 * (sources + 2) * tiles * width, transcendentals=0),
         name="moment_step",
     )(me, parts, moment, places, table)
@@ -159,21 +162,22 @@
 
 def update_kernel(kept_ref, places_ref, table_ref, out_ref):
     replicas, _, half = kept_ref.shape
-    level = lax.broadcasted_iota(jnp.int32, (block, half), 0).astype(f32)
-
-    def one_replica(r, sums):
-        values, places = kept_ref[r], places_ref[r]
-        added = []
-        for parity in range(2):
-            dense = jnp.zeros((block, half), f32)
-            for j in range(keep):
-                row = parity * keep + j
-                dense = jnp.where(places[row : row + 1] == level, values[row : row + 1], dense)
-            added.append(sums[parity] + dense)
-        return tuple(added)
-
-    empty = jnp.zeros((block, half), f32)
-    sums = lax.fori_loop(0, replicas, one_replica, (empty, empty), unroll=2)
+    sums = []
+    for parity in range(2):
+        columns = []
+        for first in range(0, half, lanes):
+            at = slice(first, min(first + lanes, half))
+            level = lax.broadcasted_iota(jnp.int32, (block, at.stop - first), 0).astype(f32)
+
+            def one_replica(r, total):
+                dense = jnp.zeros(level.shape, f32)
+                for j in range(keep):
+                    row = pl.ds(parity * keep + j, 1)
+                    dense = jnp.where(places_ref[r, row, at] == level, kept_ref[r, row, at], dense)
+                return total + dense
+
+            columns.append(lax.fori_loop(0, replicas, one_replica, jnp.zeros(level.shape, f32), unroll=4))
+        sums.append(jnp.concatenate(columns, axis=1))
     averaged = inverse(jnp.concatenate(sums, axis=0), table_ref) * (1.0 / replicas)
     squares = averaged * averaged
     high, low = halves(squares)
@@ -189,6 +193,9 @@
     return pl.pallas_call(
         update_kernel,
         out_shape=jax.ShapeDtypeStruct((half, lanes), f32),
+        in_specs=[whole] * 3,
+        out_specs=whole,
+        compiler_params=params,
         cost_estimate=pl.CostEstimate(flops=9 * replicas * lanes * half, bytes_accessed=8 * kept.size, transcendentals=lanes * half),
         name="update_step",
     )(kept, places, table)
@@ -198,7 +205,6 @@
     columns = momentum.shape[-1]
     tiles = columns // lanes
     devices = lax.axis_size("fsdp")
-    replicas = lax.axis_size("dp")
     me = lax.axis_index("fsdp")
     odd = (me % 2).reshape(1)
     grad = grad_parts[0, 0]
@@ -212,9 +218,7 @@
     kept, new_moment = moment_step(
         lax.axis_index("dp").reshape(1), parts, momentum.reshape(tiles, lanes), places, table
     )
-    everyone = lax.all_to_all(
-        jnp.broadcast_to(kept[None], (replicas,) + kept.shape), "dp", 0, 0, tiled=True
-    )
+    everyone = lax.all_to_all(kept, "dp", 0, 0, tiled=True)
     update = update_step(everyone, places, table)
     return update.reshape(1, columns), new_moment.reshape(1, 1, columns)
 

time: 79.7 us -> 70.9 us (0.89)
  Pallas kernels: 15.2 us -> 4.49 us
  waiting for transfers between devices: 24.7 us -> 28.1 us
  other arithmetic: 2.2 us -> 1.04 us
    pallas_call x2, Pallas kernels: 7.3 us -> 0.6 us  [pack(): pl.pallas_call(functools.partial(pack_kernel, other), in_specs=[pl.BlockS...]
    ppermute x1, waiting for transfers between devices: 0.01 us -> 2.11 us  [body(): arrived = lax.ppermute(sent, 'fsdp', [(i, i ^ 1) for i in range(devices)])]
    pallas_call x1, Pallas kernels: 1.91 us -> 0.24 us  [split_places(): pl.pallas_call(places_kernel, out_shape=jax.ShapeDtypeStruct((replicas, 2...]
    all_to_all x1, waiting for transfers between devices: 24.7 us -> 26 us  [body(): lax.all_to_all(own + arrived, 'fsdp', 0, 0, tiled=True, axis_index_groups...]
    pallas_call x1, Pallas kernels: 2.53 us -> 1.24 us  [moment_step(): pl.pallas_call(moment_kernel, in_specs=[pl.BlockSpec(memory_space=pltpu.S...]
    add x1, other arithmetic: 2.2 us -> 1.04 us  [body(): own + arrived]
    pallas_call x1, Pallas kernels: 3.48 us -> 2.41 us  [update_step(): pl.pallas_call(update_kernel, out_shape=jax.ShapeDtypeStruct((half, lanes...]
  transfers between devices with their start and end apart: 2 -> 2, of which waited for: 1 -> 2; matrix products, arithmetic and copies ran while one was open for 0% -> 0% of each run, Pallas kernels for 7% -> 1%
where the time goes in v2:
time: 70.9 us; the launch traced here: 70.6 us
  waiting for transfers between devices  28.1 us (40%)
  blocking collectives  22.4 us (32%)
  starting transfers between devices  12.4 us (17%)
  Pallas kernels  4.49 us (6%)
  local copies, waits for them, and re-layouts  1.51 us (2%)
  other arithmetic  1.04 us (1%)
    all_to_all x1, waiting for transfers between devices, body(): lax.all_to_all(own + arrived, 'fsdp', 0, 0, tiled=True, axis_index_groups...  26 us
    all_to_all x1, blocking collectives, body(): everyone = lax.all_to_all(kept, 'dp', 0, 0, tiled=True)  22.4 us
    all_to_all x1, starting transfers between devices, body(): lax.all_to_all(own + arrived, 'fsdp', 0, 0, tiled=True, axis_index_groups...  10.4 us
    pallas_call x1, Pallas kernels, update_step(): pl.pallas_call(update_kernel, out_shape=jax.ShapeDtypeStruct((half, lanes...  2.41 us
    ppermute x1, waiting for transfers between devices, body(): arrived = lax.ppermute(sent, 'fsdp', [(i, i ^ 1) for i in range(devices)])  2.11 us
    ppermute x1, starting transfers between devices, body(): arrived = lax.ppermute(sent, 'fsdp', [(i, i ^ 1) for i in range(devices)])  1.92 us
    unnamed x8, local copies, waits for them, and re-layouts  1.51 us
  transfers between devices with their start and end apart: 2, of which 2 were waited for; matrix products, arithmetic and copies ran while one was open for 0% of the time, Pallas kernels for 1%

profile of v2, /device:TPU:8, one launch (start us, length us, event | category | flops | bytes accessed | tf_op | source)
XLA Modules:
  0.0 70.6 jit_solution(6928745158351869075)
XLA Ops:
  0.6 0.0 copy-start
  0.7 1.5 %copy-done = f32[1,1,16,28672]{3,2,1,0:T(8,128)S(1)} copy-done((f32[1,1,16,28672]{3,2,1,0:T(8,128)S(1)}, f32[1,1,16,28672]{3,2,1,0:T(8,128)}, u32[]{:S(2)}) %copy-start) | copy-done | bytes 1835032
  2.1 0.3 pack_other.1
  2.4 1.9 %collective-permute-start = (f32[8,224,128]{2,1,0:T(8,128)S(1)}, f32[8,224,128]{2,1,0:T(8,128)S(1)}, u32[]{:S(2)}, u32[]{:S(2)}) collective-permute-start(f32[8,224,128]{2,1,0:T(8,128)S(1)} %pack_other.1), channel_id=1, source_target_pairs={{0,1},{1,0},{2,3},{3,2},{4,5},{5,4},{6,7},{7,6},{8,9},{9,8},{10,11... | collective-permute-start | bytes 2752520 | tf_op jit(solution)/shard_map/ppermute | solution.py:213
  4.4 0.3 pack_own.1
  4.7 0.0 copy-start.1
  4.7 2.1 %collective-permute-done = f32[8,224,128]{2,1,0:T(8,128)S(1)} collective-permute-done((f32[8,224,128]{2,1,0:T(8,128)S(1)}, f32[8,224,128]{2,1,0:T(8,128)S(1)}, u32[]{:S(2)}, u32[]{:S(2)}) %collective-permute-start) | collective-permute-done | bytes 917536 | tf_op jit(solution)/shard_map/ppermute | solution.py:213
  6.8 1.0 %add.8 = f32[8,224,128]{2,1,0:T(8,128)} add(f32[8,224,128]{2,1,0:T(8,128)S(1)} %pack_own.1, f32[8,224,128]{2,1,0:T(8,128)S(1)} %collective-permute-done) | non-fusion elementwise | flops 229376 | bytes 2752512 | tf_op jit(solution)/shard_map/add | solution.py:217
  7.9 0.0 copy-start.2
  7.9 0.0 copy-start.3
  7.9 10.4 %all-to-all-start = ((f32[8,224,128]{2,1,0:T(8,128)}), f32[8,224,128]{2,1,0:T(8,128)S(1)}, u32[]{:S(2)}, u32[]{:S(2)}) async-start(f32[8,224,128]{2,1,0:T(8,128)} %add.8), calls=%async_computation | async-start | bytes 1835008 | tf_op jit(solution)/shard_map/all_to_all | solution.py:217
  18.3 0.0 copy-done.1
  18.3 0.2 split_places.1.places_ref
  18.6 26.0 %all-to-all-done.parts_ref = f32[8,224,128]{2,1,0:T(8,128)S(1)} async-done(((f32[8,224,128]{2,1,0:T(8,128)}), f32[8,224,128]{2,1,0:T(8,128)S(1)}, u32[]{:S(2)}, u32[]{:S(2)}) %all-to-all-start) | async-done | bytes 917536 | tf_op jit(solution)/shard_map/all_to_all | solution.py:217
  44.5 0.0 copy-done.2
  44.5 0.0 copy-done.3
  44.5 1.2 %moment_step.1 = (f32[32,8,224]{2,1,0:T(8,128)S(1)}, f32[224,128]{1,0:T(8,128)}) custom-call(s32[1]{0:T(128)} %bitcast.me_ref, f32[8,224,128]{2,1,0:T(8,128)S(1)} %all-to-all-done.parts_ref, f32[224,128]{1,0:T(8,128)S(1)} %bitcast.10, f32[32,8,224]{2,1,0:T(8,128)S(1)} %split_places.1.places_ref, bf16[2,128,128]{2,1,0:T(8,128)(2,1)S(1)} %copy-done.2), custom_call_target="tpu_custom_call" | custom-call | flops 44040192 | bytes 1146880 | tf_op jit(solution)/shard_map/moment_step/pallas_call | solution.py:149
  45.8 22.4 %all_to_all.10.kept_ref = f32[32,8,224]{2,1,0:T(8,128)S(1)} all-to-all(f32[32,8,224]{2,1,0:T(8,128)S(1)} %get-tuple-element.4), channel_id=1, replica_groups=mesh['dp'=32,'fsdp'=16] {'dp'}, dimensions={0} | all-to-all | bytes 458752 | tf_op jit(solution)/shard_map/all_to_all | solution.py:221
  68.2 2.4 %update_step.1 = f32[224,128]{1,0:T(8,128)} custom-call(f32[32,8,224]{2,1,0:T(8,128)S(1)} %all_to_all.10.kept_ref, f32[32,8,224]{2,1,0:T(8,128)S(1)} %split_places.1.places_ref, bf16[2,128,128]{2,1,0:T(8,128)(2,1)S(1)} %copy-done.2), custom_call_target="tpu_custom_call" | custom-call | flops 8257536 | bytes 458752 | tf_op jit(solution)/shard_map/update_step/pallas_call | solution.py:193
Async XLA Ops:
  0.6 1.5 %copy-start = (f32[1,1,16,28672]{3,2,1,0:T(8,128)S(1)}, f32[1,1,16,28672]{3,2,1,0:T(8,128)}, u32[]{:S(2)}) copy-start(f32[1,1,16,28672]{3,2,1,0:T(8,128)} %param.4) | copy-start | bytes 5505028
  2.4 4.4 %collective-permute-start = (f32[8,224,128]{2,1,0:T(8,128)S(1)}, f32[8,224,128]{2,1,0:T(8,128)S(1)}, u32[]{:S(2)}, u32[]{:S(2)}) collective-permute-start(f32[8,224,128]{2,1,0:T(8,128)S(1)} %pack_other.1), channel_id=1, source_target_pairs={{0,1},{1,0},{2,3},{3,2},{4,5},{5,4},{6,7},{7,6},{8,9},{9,8},{10,11... | collective-permute-start | bytes 2752520 | tf_op jit(solution)/shard_map/ppermute | solution.py:213
  4.7 13.6 %copy-start.1 = (s32[32,1,4,448]{3,2,1,0:T(4,128)S(1)}, s32[32,1,4,448]{3,2,1,0:T(4,128)}, u32[]{:S(2)}) copy-start(s32[32,1,4,448]{3,2,1,0:T(4,128)} %param.6) | copy-start | bytes 688132
  7.9 36.7 %copy-start.2 = (bf16[2,128,128]{2,1,0:T(8,128)(2,1)S(1)}, bf16[2,128,128]{2,1,0:T(8,128)(2,1)}, u32[]{:S(2)}) copy-start(bf16[2,128,128]{2,1,0:T(8,128)(2,1)} %constant.24.clone.table_ref) | copy-start | bytes 196612
  7.9 36.7 %copy-start.3 = (f32[1,1,28672]{2,1,0:T(1,128)S(1)}, f32[1,1,28672]{2,1,0:T(1,128)}, u32[]{:S(2)}) copy-start(f32[1,1,28672]{2,1,0:T(1,128)} %param.5) | copy-start | bytes 344068
  7.9 36.7 %all-to-all-start = ((f32[8,224,128]{2,1,0:T(8,128)}), f32[8,224,128]{2,1,0:T(8,128)S(1)}, u32[]{:S(2)}, u32[]{:S(2)}) async-start(f32[8,224,128]{2,1,0:T(8,128)} %add.8), calls=%async_computation | async-start | bytes 1835008 | tf_op jit(solution)/shard_map/all_to_all | solution.py:217

commit v3 on v2

--- a/solution.py
+++ b/solution.py
@@ -119,45 +119,119 @@
     )(positions)
 
 
-def moment_kernel(me_ref, parts_ref, moment_ref, places_ref, table_ref, kept_ref, new_ref):
-    accumulated = decay_rate * moment_ref[...]
+def select(coeffs, places):
+    level = lax.broadcasted_iota(jnp.int32, (block, coeffs.shape[1]), 0).astype(f32)
+    kept = []
+    for parity in range(2):
+        mine = coeffs[parity * block : (parity + 1) * block]
+        for j in range(keep):
+            row = parity * keep + j
+            kept.append(jnp.sum(jnp.where(places[row : row + 1] == level, mine, 0.0), axis=0, keepdims=True))
+    return jnp.concatenate(kept, axis=0)
+
+
+def spread(kept, places):
+    level = lax.broadcasted_iota(jnp.int32, (block, kept.shape[1]), 0).astype(f32)
+    dense = []
+    for parity in range(2):
+        mine = jnp.zeros(level.shape, f32)
+        for j in range(keep):
+            row = parity * keep + j
+            mine = jnp.where(places[row : row + 1] == level, kept[row : row + 1], mine)
+        dense.append(mine)
+    return jnp.concatenate(dense, axis=0)
+
+
+def own_kernel(me_ref, places_ref, moment_ref, table_ref, copies_ref, kept_ref):
+    _, count, spans = places_ref.shape
+    half = spans // 2
+    source = lax.broadcasted_iota(jnp.int32, (spans, half), 0)
+    target = lax.broadcasted_iota(jnp.int32, (spans, half), 1)
+    places = places_ref[me_ref[0]].astype(f32).astype(bf16)
+    split = []
+    for parity in range(2):
+        chooser = (source == 2 * target + parity).astype(f32).astype(bf16)
+        split.append(jnp.dot(places, chooser, preferred_element_type=f32))
+    own = jnp.concatenate(split, axis=0)
+    copies_ref[...] = jnp.broadcast_to(own[None], copies_ref.shape)
+    kept_ref[...] = select(forward(decay_rate * moment_ref[...], table_ref), own)
+
+
+def own_step(me, positions, moment, table, copies):
+    replicas, count, spans = positions.shape
+    tiles = moment.shape[0]
+    return pl.pallas_call(
+        own_kernel,
+        in_specs=[pl.BlockSpec(memory_space=pltpu.SMEM), whole, whole, whole],
+        out_specs=[whole, whole],
+        out_shape=[
+            jax.ShapeDtypeStruct((copies, 2 * count, spans // 2), f32),
+            jax.ShapeDtypeStruct((2 * count, spans // 2), f32),
+        ],
+        compiler_params=params,
+        cost_estimate=pl.CostEstimate(flops=12 * moment.size * lanes, bytes_accessed=8 * moment.size, transcendentals=0),
+        name="own_step",
+    )(me, positions, moment, table)
+
+
+def share_kernel(sums_ref, places_ref, table_ref, kept_ref):
+    for row in range(sums_ref.shape[0]):
+        kept_ref[row] = select(forward(sums_ref[row], table_ref), places_ref[row])
+
+
+def share_step(sums, places, table):
+    return pl.pallas_call(
+        share_kernel,
+        in_specs=[whole, whole, whole],
+        out_specs=whole,
+        out_shape=jax.ShapeDtypeStruct(places.shape, f32),
+        compiler_params=params,
+        cost_estimate=pl.CostEstimate(flops=6 * sums.size * lanes, bytes_accessed=4 * sums.size, transcendentals=0),
+        name="share_step",
+    )(sums, places, table)
+
+
+def kept_kernel(shares_ref, kept_ref, copies_ref, out_ref):
+    total = kept_ref[...]
+    for source in range(shares_ref.shape[0]):
+        total = total + shares_ref[source]
+    out_ref[...] = total
+    copies_ref[...] = jnp.broadcast_to(total[None], copies_ref.shape)
+
+
+def kept_step(shares, kept, replicas):
+    return pl.pallas_call(
+        kept_kernel,
+        in_specs=[whole, whole],
+        out_specs=[whole, whole],
+        out_shape=[
+            jax.ShapeDtypeStruct((replicas,) + kept.shape, f32),
+            jax.ShapeDtypeStruct(kept.shape, f32),
+        ],
+        compiler_params=params,
+        cost_estimate=pl.CostEstimate(flops=shares.size, bytes_accessed=4 * shares.size, transcendentals=0),
+        name="kept_step",
+    )(shares, kept)
+
+
+def moment_kernel(parts_ref, moment_ref, kept_ref, places_ref, table_ref, new_ref):
     gradient = parts_ref[0]
     for source in range(1, parts_ref.shape[0]):
         gradient = gradient + parts_ref[source]
-    accumulated = accumulated + gradient
-    coeffs = forward(accumulated, table_ref)
-    half = coeffs.shape[1]
-    level = lax.broadcasted_iota(jnp.int32, (block, half), 0).astype(f32)
-    own = places_ref[me_ref[0]]
-    dense, kept = [], []
-    for parity in range(2):
-        mine = coeffs[parity * block : (parity + 1) * block]
-        inside = jnp.zeros_like(mine)
-        for j in range(keep):
-            row = parity * keep + j
-            picked = jnp.where(own[row : row + 1] == level, mine, 0.0)
-            inside = inside + picked
-            kept.append(jnp.sum(picked, axis=0, keepdims=True))
-        dense.append(inside)
-    kept_ref[...] = jnp.broadcast_to(jnp.concatenate(kept, axis=0)[None], kept_ref.shape)
-    new_ref[...] = accumulated - inverse(jnp.concatenate(dense, axis=0), table_ref)
-
-
-def moment_step(me, parts, moment, places, table):
-    replicas = places.shape[0]
-    sources, tiles, width = parts.shape
+    dense = spread(kept_ref[...], places_ref[0])
+    new_ref[...] = decay_rate * moment_ref[...] + gradient - inverse(dense, table_ref)
+
+
+def moment_step(parts, moment, kept, places, table):
     return pl.pallas_call(
         moment_kernel,
-        in_specs=[pl.BlockSpec(memory_space=pltpu.SMEM), whole, whole, whole, whole],
-        out_specs=[whole, whole],
-        out_shape=[
-            jax.ShapeDtypeStruct((replicas, 2 * keep, tiles), f32),
-            jax.ShapeDtypeStruct((tiles, width), f32),
-        ],
-        compiler_params=params,
-        cost_estimate=pl.CostEstimate(flops=12 * tiles * width * width, bytes_accessed=4 * (sources + 2) * tiles * width, transcendentals=0),
+        in_specs=[whole] * 5,
+        out_specs=whole,
+        out_shape=jax.ShapeDtypeStruct(moment.shape, f32),
+        compiler_params=params,
+        cost_estimate=pl.CostEstimate(flops=6 * moment.size * lanes, bytes_accessed=4 * parts.size, transcendentals=0),
         name="moment_step",
-    )(me, parts, moment, places, table)
+    )(parts, moment, kept, places, table)
 
 
 def update_kernel(kept_ref, places_ref, table_ref, out_ref):
@@ -209,17 +283,23 @@
     odd = (me % 2).reshape(1)
     grad = grad_parts[0, 0]
     table = jnp.asarray(split_table())
-    sent = pack(grad, odd, True)
-    arrived = lax.ppermute(sent, "fsdp", [(i, i ^ 1) for i in range(devices)])
-    own = pack(grad, odd, False)
-    places = split_places(positions[:, 0])
     groups = [list(range(core, devices, 2)) for core in range(2)]
-    parts = lax.all_to_all(own + arrived, "fsdp", 0, 0, tiled=True, axis_index_groups=groups)
-    kept, new_moment = moment_step(
-        lax.axis_index("dp").reshape(1), parts, momentum.reshape(tiles, lanes), places, table
-    )
-    everyone = lax.all_to_all(kept, "dp", 0, 0, tiled=True)
-    update = update_step(everyone, places, table)
+
+    def along_z(x):
+        return lax.all_to_all(x, "fsdp", 0, 0, tiled=True, axis_index_groups=groups)
+
+    moment = momentum.reshape(tiles, lanes)
+    positions = positions[:, 0]
+    own_places, own_kept = own_step(lax.axis_index("dp").reshape(1), positions, moment, table, devices // 2)
+    arrived = lax.ppermute(pack(grad, odd, True), "fsdp", [(i, i ^ 1) for i in range(devices)])
+    row_places = along_z(own_places)
+    sums = pack(grad, odd, False) + arrived
+    gradient = lax.psum_scatter(sums, "fsdp", scatter_dimension=0, tiled=True, axis_index_groups=groups)
+    shares = along_z(share_step(sums, row_places, table))
+    copies, kept = kept_step(shares, own_kept, positions.shape[0])
+    everyone = lax.all_to_all(copies, "dp", 0, 0, tiled=True)
+    new_moment = moment_step(gradient.reshape(1, tiles, lanes), moment, kept, own_places, table)
+    update = update_step(everyone, split_places(positions), table)
     return update.reshape(1, columns), new_moment.reshape(1, 1, columns)
 
 

time: 70.9 us -> 79 us (1.11)
  waiting for transfers between devices: 28.1 us -> 12.9 us
  between operations: 0.69 us -> 14.2 us
  blocking collectives: 22.4 us -> 29.4 us
  Pallas kernels: 4.49 us -> 6.54 us
  local copies, waits for them, and re-layouts: 1.51 us -> 2.41 us
    all_to_all x1, waiting for transfers between devices: 26 us -> 10.8 us  [body(): everyone = lax.all_to_all(copies, 'dp', 0, 0, tiled=True)]
    all_to_all x1 -> x2, blocking collectives: 22.4 us -> 29.4 us  [along_z(): return lax.all_to_all(x, 'fsdp', 0, 0, tiled=True, axis_index_groups=groups)]
    pallas_call x1 -> x4, Pallas kernels: 1.24 us -> 3.29 us  [the longest x1 1.29 us: share_step(): pl.pallas_call(share_kernel, in_specs=[whole, whole, whole], out_specs=wh...]
    unnamed x8 -> x12, local copies, waits for them, and re-layouts: 1.51 us -> 2.41 us
  transfers between devices with their start and end apart: 2 -> 3, of which waited for: 2 -> 2; matrix products, arithmetic and copies ran while one was open for 0% -> 0% of each run, Pallas kernels for 1% -> 7%
where the time goes in v3:
time: 79 us; the launch traced here: 78.6 us
  blocking collectives  29.4 us (37%)
  between operations  14.2 us (18%)
  waiting for transfers between devices  12.9 us (16%)
  starting transfers between devices  12.2 us (15%)
  Pallas kernels  6.54 us (8%)
  local copies, waits for them, and re-layouts  2.41 us (3%)
  other arithmetic  1.02 us (1%)
    all_to_all x2, blocking collectives, along_z(): return lax.all_to_all(x, 'fsdp', 0, 0, tiled=True, axis_index_groups=groups)  29.4 us
    all_to_all x1, waiting for transfers between devices, body(): everyone = lax.all_to_all(copies, 'dp', 0, 0, tiled=True)  10.8 us
    all_to_all x1, starting transfers between devices, body(): everyone = lax.all_to_all(copies, 'dp', 0, 0, tiled=True)  10.2 us
    unnamed x12, local copies, waits for them, and re-layouts  2.41 us
    pallas_call x1, Pallas kernels, update_step(): pl.pallas_call(update_kernel, out_shape=jax.ShapeDtypeStruct((half, lanes...  2.41 us
    ppermute x1, waiting for transfers between devices, body(): lax.ppermute(pack(grad, odd, True), 'fsdp', [(i, i ^ 1) for i in range(de...  2.09 us
    ppermute x1, starting transfers between devices, body(): lax.ppermute(pack(grad, odd, True), 'fsdp', [(i, i ^ 1) for i in range(de...  1.92 us
  transfers between devices with their start and end apart: 3, of which 2 were waited for; matrix products, arithmetic and copies ran while one was open for 0% of the time, Pallas kernels for 7%

profile of v3, /device:TPU:8, one launch (start us, length us, event | category | flops | bytes accessed | tf_op | source)
XLA Modules:
  0.0 78.6 jit_solution(13380124766076070874)
XLA Ops:
  7.2 0.0 reduce-scatter.2.cloned.1.call-start
  7.2 0.0 copy-start.1
  7.2 1.5 %copy-done.1 = f32[1,1,16,28672]{3,2,1,0:T(8,128)S(1)} copy-done((f32[1,1,16,28672]{3,2,1,0:T(8,128)S(1)}, f32[1,1,16,28672]{3,2,1,0:T(8,128)}, u32[]{:S(2)}) %copy-start.1) | copy-done | bytes 1835032
  8.7 0.3 pack_other.1
  9.0 1.9 %collective-permute-start = (f32[8,224,128]{2,1,0:T(8,128)S(1)}, f32[8,224,128]{2,1,0:T(8,128)S(1)}, u32[]{:S(2)}, u32[]{:S(2)}) collective-permute-start(f32[8,224,128]{2,1,0:T(8,128)S(1)} %pack_other.1), channel_id=1, source_target_pairs={{0,1},{1,0},{2,3},{3,2},{4,5},{5,4},{6,7},{7,6},{8,9},{9,8},{10,11... | collective-permute-start | bytes 2752520 | tf_op jit(solution)/shard_map/ppermute | solution.py:294
  11.0 0.3 pack_own.1
  11.3 0.0 copy-start.2
  11.3 0.0 copy-start.3
  11.3 0.0 copy-start.4
  11.3 2.1 %collective-permute-done = f32[8,224,128]{2,1,0:T(8,128)S(1)} collective-permute-done((f32[8,224,128]{2,1,0:T(8,128)S(1)}, f32[8,224,128]{2,1,0:T(8,128)S(1)}, u32[]{:S(2)}, u32[]{:S(2)}) %collective-permute-start) | collective-permute-done | bytes 917536 | tf_op jit(solution)/shard_map/ppermute | solution.py:294
  13.4 1.0 %add.10.sums_ref = f32[8,224,128]{2,1,0:T(8,128)} add(f32[8,224,128]{2,1,0:T(8,128)S(1)} %pack_own.1, f32[8,224,128]{2,1,0:T(8,128)S(1)} %collective-permute-done) | non-fusion elementwise | flops 229376 | bytes 2752512 | tf_op jit(solution)/shard_map/add | solution.py:296
  14.4 0.0 copy-start
  14.4 0.0 reduce-scatter.2.cloned.1.call-update
  14.4 0.0 copy-done.2
  14.5 0.0 copy-done.3
  14.5 0.0 copy-done.4
  14.5 0.4 own_step.1
  14.9 18.5 %all_to_all.15.places_ref = f32[8,8,224]{2,1,0:T(8,128)S(1)} all-to-all(f32[8,8,224]{2,1,0:T(8,128)S(1)} %get-tuple-element.6.places_ref), channel_id=1, replica_groups={{0,2,4,6,8,10,12,14},{1,3,5,7,9,11,13,15},{16,18,20,22,24,26,28,30},{17..., dimensions={0} | all-to-all | bytes 114688 | tf_op jit(solution)/shard_map/all_to_all | solution.py:289
  33.3 0.0 copy-done
  33.3 1.3 %share_step.1 = f32[8,8,224]{2,1,0:T(8,128)S(1)} custom-call(f32[8,224,128]{2,1,0:T(8,128)S(1)} %copy-done, f32[8,8,224]{2,1,0:T(8,128)S(1)} %all_to_all.15.places_ref, bf16[2,128,128]{2,1,0:T(8,128)(2,1)S(1)} %copy-done.3), custom_call_target="tpu_custom_call" | custom-call | flops 176160768 | bytes 917504 | tf_op jit(solution)/shard_map/share_step/pallas_call | solution.py:183
  34.7 10.9 %all_to_all.16.shares_ref = f32[8,8,224]{2,1,0:T(8,128)S(1)} all-to-all(f32[8,8,224]{2,1,0:T(8,128)S(1)} %share_step.1), channel_id=1, replica_groups={{0,2,4,6,8,10,12,14},{1,3,5,7,9,11,13,15},{16,18,20,22,24,26,28,30},{17..., dimensions={0} | all-to-all | bytes 114688 | tf_op jit(solution)/shard_map/all_to_all | solution.py:289
  45.6 0.7 kept_step.1
  46.3 10.2 %all-to-all-start.2 = ((f32[32,8,224]{2,1,0:T(8,128)}), f32[32,8,224]{2,1,0:T(8,128)S(1)}, u32[]{:S(2)}, u32[]{:S(2)}) async-start(f32[32,8,224]{2,1,0:T(8,128)} %get-tuple-element.8), calls=%async_computation.2 | async-start | bytes 524288 | tf_op jit(solution)/shard_map/all_to_all | solution.py:300
  56.5 0.2 split_places.1.places_ref
  56.8 10.8 %all-to-all-done.2.kept_ref = f32[32,8,224]{2,1,0:T(8,128)S(1)} async-done(((f32[32,8,224]{2,1,0:T(8,128)}), f32[32,8,224]{2,1,0:T(8,128)S(1)}, u32[]{:S(2)}, u32[]{:S(2)}) %all-to-all-start.2) | async-done | bytes 229408 | tf_op jit(solution)/shard_map/all_to_all | solution.py:300
  67.6 2.4 %update_step.1 = f32[224,128]{1,0:T(8,128)} custom-call(f32[32,8,224]{2,1,0:T(8,128)S(1)} %all-to-all-done.2.kept_ref, f32[32,8,224]{2,1,0:T(8,128)S(1)} %split_places.1.places_ref, bf16[2,128,128]{2,1,0:T(8,128)(2,1)S(1)} %copy-done.3), custom_call_target="tpu_custom_call" | custom-call | flops 8257536 | bytes 458752 | tf_op jit(solution)/shard_map/update_step/pallas_call | solution.py:267
  70.0 0.0 reduce-scatter.2.cloned.1.call-done.parts_ref
  70.0 0.0 copy-start.5
  70.0 0.9 %copy-done.5 = f32[1,224,128]{2,1,0:T(8,128)S(1)} copy-done((f32[1,224,128]{2,1,0:T(8,128)S(1)}, f32[1,224,128]{2,1,0:T(8,128)}, u32[]{:S(2)}) %copy-start.5) | copy-done | bytes 114712
  70.9 0.9 %moment_step.1 = f32[224,128]{1,0:T(8,128)} custom-call(f32[1,224,128]{2,1,0:T(8,128)S(1)} %copy-done.5, f32[224,128]{1,0:T(8,128)S(1)} %bitcast.12, f32[8,224]{1,0:T(8,128)S(1)} %get-tuple-element.9.kept_ref, f32[8,8,224]{2,1,0:T(8,128)S(1)} %get-tuple-element.6.places_ref, bf16[2,128,128]{2,1,0:T(8,128)(2,1)S(1)} %copy-done.3), custom_call_target="tpu_custom_call" | custom-call | flops 22020096 | bytes 114688 | tf_op jit(solution)/shard_map/moment_step/pallas_call | solution.py:226
Async XLA Ops:
  7.2 62.8 %reduce-scatter.2.cloned.1.call-start = ((), (), s32[]{:S(2)}) async-start(), calls=%async_computation.4 | async-start | bytes 1032192 | tf_op jit(solution)/shard_map/reduce_scatter | solution.py:297
  7.2 1.5 %copy-start.1 = (f32[1,1,16,28672]{3,2,1,0:T(8,128)S(1)}, f32[1,1,16,28672]{3,2,1,0:T(8,128)}, u32[]{:S(2)}) copy-start(f32[1,1,16,28672]{3,2,1,0:T(8,128)} %param.4) | copy-start | bytes 5505028
  9.0 4.4 %collective-permute-start = (f32[8,224,128]{2,1,0:T(8,128)S(1)}, f32[8,224,128]{2,1,0:T(8,128)S(1)}, u32[]{:S(2)}, u32[]{:S(2)}) collective-permute-start(f32[8,224,128]{2,1,0:T(8,128)S(1)} %pack_other.1), channel_id=1, source_target_pairs={{0,1},{1,0},{2,3},{3,2},{4,5},{5,4},{6,7},{7,6},{8,9},{9,8},{10,11... | collective-permute-start | bytes 2752520 | tf_op jit(solution)/shard_map/ppermute | solution.py:294
  11.3 3.2 %copy-start.2 = (s32[32,1,4,448]{3,2,1,0:T(4,128)S(1)}, s32[32,1,4,448]{3,2,1,0:T(4,128)}, u32[]{:S(2)}) copy-start(s32[32,1,4,448]{3,2,1,0:T(4,128)} %param.6) | copy-start | bytes 688132
  11.3 3.2 %copy-start.3 = (bf16[2,128,128]{2,1,0:T(8,128)(2,1)S(1)}, bf16[2,128,128]{2,1,0:T(8,128)(2,1)}, u32[]{:S(2)}) copy-start(bf16[2,128,128]{2,1,0:T(8,128)(2,1)} %constant.24.clone.table_ref) | copy-start | bytes 196612
  11.3 3.2 %copy-start.4 = (f32[1,1,28672]{2,1,0:T(1,128)S(1)}, f32[1,1,28672]{2,1,0:T(1,128)}, u32[]{:S(2)}) copy-start(f32[1,1,28672]{2,1,0:T(1,128)} %param.5) | copy-start | bytes 344068
  14.4 18.9 %copy-start = (f32[8,224,128]{2,1,0:T(8,128)S(1)}, f32[8,224,128]{2,1,0:T(8,128)}, u32[]{:S(2)}) copy-start(f32[8,224,128]{2,1,0:T(8,128)} %add.10.sums_ref) | copy-start | bytes 2752516
  46.3 21.3 %all-to-all-start.2 = ((f32[32,8,224]{2,1,0:T(8,128)}), f32[32,8,224]{2,1,0:T(8,128)S(1)}, u32[]{:S(2)}, u32[]{:S(2)}) async-start(f32[32,8,224]{2,1,0:T(8,128)} %get-tuple-element.8), calls=%async_computation.2 | async-start | bytes 524288 | tf_op jit(solution)/shard_map/all_to_all | solution.py:300
  70.0 0.9 %copy-start.5 = (f32[1,224,128]{2,1,0:T(8,128)S(1)}, f32[1,224,128]{2,1,0:T(8,128)}, u32[]{:S(2)}) copy-start(f32[1,224,128]{2,1,0:T(8,128)} %reduce-scatter.2.cloned.1.call-done.parts_ref) | copy-start | bytes 344068
Sparse Core Ops, SparseCore 0:
  14.6 46.3 reduce-scatter.1

commit v4 on v2

v4 whole, which is shorter than its diff:
```python
import functools

import jax
import jax.numpy as jnp
import numpy as np
from jax import lax
from jax.experimental import pallas as pl
from jax.experimental.pallas import tpu as pltpu
from jax.sharding import PartitionSpec as P

decay_rate = 0.999
epsilon = 1e-06
block = 64
lanes = 128
keep = 4
f32, bf16 = jnp.float32, jnp.bfloat16
whole = pl.BlockSpec(memory_space=pltpu.VMEM)
smem = pl.BlockSpec(memory_space=pltpu.SMEM)
params = pltpu.CompilerParams(vmem_limit_bytes=12 * 2**20)


def paired_table():
    frequency = np.arange(block)[:, None]
    sample = np.arange(block)[None, :]
    cosines = np.cos(np.pi * (2.0 * sample + 1.0) * frequency / (2.0 * block))
    norming = np.where(frequency == 0, np.sqrt(1.0 / block), np.sqrt(2.0 / block))
    return np.kron(np.eye(2), cosines * norming).astype(np.float32)


def tables():
    table = paired_table()
    high = table.astype(jnp.bfloat16)
    low = (table - high.astype(np.float32)).astype(jnp.bfloat16)
    none = np.zeros_like(high)
    ones = np.kron(np.eye(2), np.ones((block, block))).astype(jnp.bfloat16)
    return (
        np.block([[high, high], [low, none]]),
        np.block([[high, low], [high, none]]),
        np.concatenate([ones, ones]),
    )


def halves(x):
    high = x.astype(bf16)
    return high, (x - high.astype(f32)).astype(bf16)


def forward(fields, table_ref):
    parts = jnp.concatenate(halves(fields), axis=1)
    both = lax.dot_general(table_ref[...], parts, (((1,), (1,)), ((), ())), preferred_element_type=f32)
    return both[:lanes] + both[lanes:]


def inverse(coeffs, table_ref):
    parts = jnp.concatenate(halves(coeffs), axis=0)
    both = lax.dot_general(parts, table_ref[...], (((0,), (0,)), ((), ())), preferred_element_type=f32)
    return both[:, :lanes] + both[:, lanes:]


def block_sums(coeffs, ones_ref):
    parts = jnp.concatenate(halves(coeffs), axis=0)
    return lax.dot_general(parts, ones_ref[...], (((0,), (0,)), ((), ())), preferred_element_type=f32)


def same_core_rows(x, odd):
    upper, lower = x[:8], x[8:]
    row = lax.broadcasted_iota(jnp.int32, upper.shape, 0)
    even_place = row % 2 == 0
    return jnp.where(
        odd,
        jnp.where(even_place, pltpu.roll(upper, 7, 0), lower),
        jnp.where(even_place, upper, pltpu.roll(lower, 1, 0)),
    )


def pack_kernel(other, odd_ref, grad_ref, out_ref):
    odd = (odd_ref[0] != 0) != other
    for first in range(0, out_ref.shape[1], 8):
        mixed = jnp.stack(
            [
                same_core_rows(grad_ref[:, tile * lanes : (tile + 1) * lanes], odd)
                for tile in range(first, first + 8)
            ]
        )
        rows = jnp.swapaxes(mixed, 0, 1)
        for place in range(8):
            out_ref[place // 2 + 4 * (place % 2), first : first + 8, :] = rows[place]


def pack(grad, odd, other):
    rows, columns = grad.shape
    return pl.pallas_call(
        functools.partial(pack_kernel, other),
        in_specs=[smem, whole],
        out_specs=whole,
        out_shape=jax.ShapeDtypeStruct((rows // 2, columns // lanes, lanes), f32),
        compiler_params=params,
        cost_estimate=pl.CostEstimate(flops=rows * columns, bytes_accessed=6 * rows * columns, transcendentals=0),
        name="pack_other" if other else "pack_own",
    )(odd, grad)


def places_kernel(places_ref, out_ref):
    replicas, count, spans = places_ref.shape
    half = spans // 2
    source = lax.broadcasted_iota(jnp.int32, (spans, half), 0)
    target = lax.broadcasted_iota(jnp.int32, (spans, half), 1)
    places = places_ref[...].reshape(replicas * count, spans).astype(f32).astype(bf16)
    for parity in range(2):
        chooser = (source == 2 * target + parity).astype(f32).astype(bf16)
        chosen = jnp.dot(places, chooser, preferred_element_type=f32)
        out_ref[:, parity * count : (parity + 1) * count, :] = chosen.reshape(replicas, count, half)


def split_places(positions):
    replicas, count, spans = positions.shape
    return pl.pallas_call(
        places_kernel,
        out_shape=jax.ShapeDtypeStruct((replicas, 2 * count, spans // 2), f32),
        in_specs=[whole],
        out_specs=whole,
        compiler_params=params,
        cost_estimate=pl.CostEstimate(flops=2 * replicas * count * spans * spans, bytes_accessed=8 * replicas * count * spans, transcendentals=0),
        name="split_places",
    )(positions)


def kept_kernel(me_ref, parts_ref, moment_ref, places_ref, table_ref, copies_ref, accumulated_ref):
    gradient = parts_ref[0]
    for source in range(1, parts_ref.shape[0]):
        gradient = gradient + parts_ref[source]
    accumulated = decay_rate * moment_ref[...] + gradient
    accumulated_ref[...] = accumulated
    coeffs = forward(accumulated, table_ref)
    level = lax.broadcasted_iota(jnp.int32, (block, coeffs.shape[1]), 0).astype(f32)
    own = places_ref[me_ref[0]]
    kept = []
    for parity in range(2):
        mine = coeffs[parity * block : (parity + 1) * block]
        for j in range(keep):
            row = parity * keep + j
            kept.append(jnp.sum(jnp.where(own[row : row + 1] == level, mine, 0.0), axis=0, keepdims=True))
    copies_ref[...] = jnp.broadcast_to(jnp.concatenate(kept, axis=0)[None], copies_ref.shape)


def kept_step(me, parts, moment, places, table):
    return pl.pallas_call(
        kept_kernel,
        in_specs=[smem] + [whole] * 4,
        out_specs=[whole, whole],
        out_shape=[
            jax.ShapeDtypeStruct(places.shape, f32),
            jax.ShapeDtypeStruct(moment.shape, f32),
        ],
        compiler_params=params,
        cost_estimate=pl.CostEstimate(flops=6 * moment.size * lanes, bytes_accessed=4 * parts.size, transcendentals=0),
        name="kept_step",
    )(me, parts, moment, places, table)


def dense_of(kept_ref, places_ref, replica, parity, at, level):
    dense = jnp.zeros(level.shape, f32)
    for j in range(keep):
        row = pl.ds(parity * keep + j, 1)
        dense = jnp.where(places_ref[replica, row, at] == level, kept_ref[replica, row, at], dense)
    return dense


def outputs_kernel(me_ref, kept_ref, places_ref, accumulated_ref, table_ref, ones_ref, update_ref, moment_ref):
    replicas, _, half = kept_ref.shape
    for first in range(0, half, lanes):
        at = slice(first, min(first + lanes, half))
        level = lax.broadcasted_iota(jnp.int32, (block, at.stop - first), 0).astype(f32)
        own, sums = [], []
        for parity in range(2):
            own.append(dense_of(kept_ref, places_ref, me_ref[0], parity, at, level))
            total = jnp.zeros(level.shape, f32)
            for replica in range(replicas):
                total = total + dense_of(kept_ref, places_ref, replica, parity, at, level)
            sums.append(total * (1.0 / replicas))
        moment_ref[at, :] = accumulated_ref[at, :] - inverse(jnp.concatenate(own, axis=0), table_ref)
        mean = jnp.concatenate(sums, axis=0)
        averaged = inverse(mean, table_ref)
        meansq = block_sums(mean * mean, ones_ref) * (1.0 / block)
        update_ref[at, :] = averaged * lax.rsqrt(averaged * averaged + meansq + epsilon)


def outputs_step(me, kept, places, accumulated, table, ones):
    replicas, _, half = kept.shape
    return pl.pallas_call(
        outputs_kernel,
        in_specs=[smem] + [whole] * 5,
        out_specs=[whole, whole],
        out_shape=[jax.ShapeDtypeStruct(accumulated.shape, f32)] * 2,
        compiler_params=params,
        cost_estimate=pl.CostEstimate(flops=9 * replicas * lanes * half, bytes_accessed=8 * kept.size, transcendentals=lanes * half),
        name="outputs_step",
    )(me, kept, places, accumulated, table, ones)


def body(grad_parts, momentum, positions):
    columns = momentum.shape[-1]
    tiles = columns // lanes
    devices = lax.axis_size("fsdp")
    me = lax.axis_index("fsdp")
    odd = (me % 2).reshape(1)
    grad = grad_parts[0, 0]
    forward_table, inverse_table, ones = (jnp.asarray(table) for table in tables())
    replica = lax.axis_index("dp").reshape(1)
    sent = pack(grad, odd, True)
    arrived = lax.ppermute(sent, "fsdp", [(i, i ^ 1) for i in range(devices)])
    own = pack(grad, odd, False)
    places = split_places(positions[:, 0])
    own, places, arrived, replica = lax.optimization_barrier((own, places, arrived, replica))
    groups = [list(range(core, devices, 2)) for core in range(2)]
    parts = lax.all_to_all(own + arrived, "fsdp", 0, 0, tiled=True, axis_index_groups=groups)
    copies, accumulated = kept_step(replica, parts, momentum.reshape(tiles, lanes), places, forward_table)
    everyone = lax.all_to_all(copies, "dp", 0, 0, tiled=True)
    update, new_moment = outputs_step(replica, everyone, places, accumulated, inverse_table, ones)
    return update.reshape(1, columns), new_moment.reshape(1, 1, columns)


def solution(mesh):
    in_specs = (P("dp", "fsdp", None, None), P("dp", "fsdp", None), P(None, "fsdp", None, None))
    out_specs = (P("fsdp", None), P("dp", "fsdp", None))
    return jax.shard_map(body, mesh=mesh, in_specs=in_specs, out_specs=out_specs, check_vma=False)
```

time: 70.9 us -> 67.5 us (0.952)
  blocking collectives: 22.4 us -> 57.6 us
  waiting for transfers between devices: 28.1 us -> 1.86 us
  starting transfers between devices: 12.4 us -> 2.05 us
  Pallas kernels: 4.49 us -> 3.34 us
  other arithmetic: 1.04 us -> 0.09 us
    all_to_all x1 -> x2, blocking collectives: 22.4 us -> 57.6 us  [the longest x1 36.5 us: body(): lax.all_to_all(own + arrived, 'fsdp', 0, 0, tiled=True, axis_index_groups...]
    all_to_all x1 -> x0, waiting for transfers between devices: 26 us -> none  [body(): lax.all_to_all(own + arrived, 'fsdp', 0, 0, tiled=True, axis_index_groups...]
    all_to_all x1 -> x0, starting transfers between devices: 10.4 us -> none  [body(): lax.all_to_all(own + arrived, 'fsdp', 0, 0, tiled=True, axis_index_groups...]
    pallas_call x4, Pallas kernels: 4.25 us -> 3.09 us  [the longest x1 2.19 us: outputs_step(): pl.pallas_call(outputs_kernel, in_specs=[smem] + [whole] * 5, out_specs=[...]
    add x1, other arithmetic: 1.04 us -> 0.09 us  [body(): own + arrived]
    unnamed x8 -> x12, local copies, waits for them, and re-layouts: 1.51 us -> 1.52 us
  transfers between devices with their start and end apart: 2 -> 1, of which waited for: 2 -> 1; matrix products, arithmetic and copies ran while one was open for 0% -> 0% of each run, Pallas kernels for 1% -> 1%
where the time goes in v4:
time: 67.5 us; the launch traced here: 67.2 us
  blocking collectives  57.6 us (85%)
  Pallas kernels  3.34 us (5%)
  starting transfers between devices  2.05 us (3%)
  waiting for transfers between devices  1.86 us (3%)
  local copies, waits for them, and re-layouts  1.52 us (2%)
  between operations  0.73 us (1%)
    all_to_all x1, blocking collectives, body(): lax.all_to_all(own + arrived, 'fsdp', 0, 0, tiled=True, axis_index_groups...  36.5 us
    all_to_all x1, blocking collectives, body(): everyone = lax.all_to_all(copies, 'dp', 0, 0, tiled=True)  21.2 us
    pallas_call x1, Pallas kernels, outputs_step(): pl.pallas_call(outputs_kernel, in_specs=[smem] + [whole] * 5, out_specs=[...  2.19 us
    ppermute x1, starting transfers between devices, body(): arrived = lax.ppermute(sent, 'fsdp', [(i, i ^ 1) for i in range(devices)])  2.05 us
    ppermute x1, waiting for transfers between devices, body(): arrived = lax.ppermute(sent, 'fsdp', [(i, i ^ 1) for i in range(devices)])  1.86 us
    unnamed x12, local copies, waits for them, and re-layouts  1.52 us
  transfers between devices with their start and end apart: 1, of which 1 were waited for; matrix products, arithmetic and copies ran while one was open for 0% of the time, Pallas kernels for 1%

profile of v4, /device:TPU:8, one launch (start us, length us, event | category | flops | bytes accessed | tf_op | source)
XLA Modules:
  0.0 67.2 jit_solution(3346010961545864731)
XLA Ops:
  0.6 0.0 copy-start
  0.7 1.5 %copy-done = f32[1,1,16,28672]{3,2,1,0:T(8,128)S(1)} copy-done((f32[1,1,16,28672]{3,2,1,0:T(8,128)S(1)}, f32[1,1,16,28672]{3,2,1,0:T(8,128)}, u32[]{:S(2)}) %copy-start) | copy-done | bytes 1835032
  2.1 0.3 pack_other.1
  2.4 0.0 copy-start.1
  2.5 2.1 %collective-permute-start = (f32[8,224,128]{2,1,0:T(8,128)S(1)}, f32[8,224,128]{2,1,0:T(8,128)S(1)}, u32[]{:S(2)}, u32[]{:S(2)}) collective-permute-start(f32[8,224,128]{2,1,0:T(8,128)S(1)} %pack_other.1), channel_id=1, source_target_pairs={{0,1},{1,0},{2,3},{3,2},{4,5},{5,4},{6,7},{7,6},{8,9},{9,8},{10,11... | collective-permute-start | bytes 2752520 | tf_op jit(solution)/shard_map/ppermute | solution.py:211
  4.5 0.3 pack_own.1
  4.8 0.0 copy-done.1
  4.8 0.2 split_places.1.places_ref
  5.1 1.9 %collective-permute-done = f32[8,224,128]{2,1,0:T(8,128)S(1)} collective-permute-done((f32[8,224,128]{2,1,0:T(8,128)S(1)}, f32[8,224,128]{2,1,0:T(8,128)S(1)}, u32[]{:S(2)}, u32[]{:S(2)}) %collective-permute-start) | collective-permute-done | bytes 917536 | tf_op jit(solution)/shard_map/ppermute | solution.py:211
  7.0 0.0 copy-start.3
  7.0 0.0 copy-start.4
  7.0 0.1 add.8
  7.1 0.0 copy-start.2
  7.1 0.0 copy-start.5
  7.1 36.5 %all_to_all.10.parts_ref = f32[8,224,128]{2,1,0:T(8,128)S(1)} all-to-all(f32[8,224,128]{2,1,0:T(8,128)S(1)} %add.8), channel_id=1, replica_groups={{0,2,4,6,8,10,12,14},{1,3,5,7,9,11,13,15},{16,18,20,22,24,26,28,30},{17..., dimensions={0} | all-to-all | bytes 1835008 | tf_op jit(solution)/shard_map/all_to_all | solution.py:216
  43.6 0.0 copy-done.3
  43.6 0.0 copy-done.4
  43.6 0.3 kept_step.1
  43.9 21.2 %all_to_all.11.kept_ref = f32[32,8,224]{2,1,0:T(8,128)S(1)} all-to-all(f32[32,8,224]{2,1,0:T(8,128)S(1)} %get-tuple-element.14), channel_id=1, replica_groups=mesh['dp'=32,'fsdp'=16] {'dp'}, dimensions={0} | all-to-all | bytes 458752 | tf_op jit(solution)/shard_map/all_to_all | solution.py:218
  65.0 0.0 copy-done.2
  65.0 0.0 copy-done.5
  65.0 2.2 %outputs_step.1 = (f32[224,128]{1,0:T(8,128)}, f32[224,128]{1,0:T(8,128)}) custom-call(s32[1]{0:T(128)} %bitcast.3.me_ref, f32[32,8,224]{2,1,0:T(8,128)S(1)} %all_to_all.11.kept_ref, f32[32,8,224]{2,1,0:T(8,128)S(1)} %split_places.1.places_ref, f32[224,128]{1,0:T(8,128)S(1)} %get-tuple-element.15.accumulated_ref, bf16[256,256]{1,0:T(8,128)(2,1)S(1)} %copy-done.2, ...), custom_call_target="tpu_custom_call" | custom-call | flops 8257536 | bytes 458752 | tf_op jit(solution)/shard_map/outputs_step/pallas_call | solution.py:190
Async XLA Ops:
  0.6 1.5 %copy-start = (f32[1,1,16,28672]{3,2,1,0:T(8,128)S(1)}, f32[1,1,16,28672]{3,2,1,0:T(8,128)}, u32[]{:S(2)}) copy-start(f32[1,1,16,28672]{3,2,1,0:T(8,128)} %param.6) | copy-start | bytes 5505028
  2.4 2.4 %copy-start.1 = (s32[32,1,4,448]{3,2,1,0:T(4,128)S(1)}, s32[32,1,4,448]{3,2,1,0:T(4,128)}, u32[]{:S(2)}) copy-start(s32[32,1,4,448]{3,2,1,0:T(4,128)} %param.8) | copy-start | bytes 688132
  2.5 4.5 %collective-permute-start = (f32[8,224,128]{2,1,0:T(8,128)S(1)}, f32[8,224,128]{2,1,0:T(8,128)S(1)}, u32[]{:S(2)}, u32[]{:S(2)}) collective-permute-start(f32[8,224,128]{2,1,0:T(8,128)S(1)} %pack_other.1), channel_id=1, source_target_pairs={{0,1},{1,0},{2,3},{3,2},{4,5},{5,4},{6,7},{7,6},{8,9},{9,8},{10,11... | collective-permute-start | bytes 2752520 | tf_op jit(solution)/shard_map/ppermute | solution.py:211
  7.0 36.6 %copy-start.3 = (bf16[256,256]{1,0:T(8,128)(2,1)S(1)}, bf16[256,256]{1,0:T(8,128)(2,1)}, u32[]{:S(2)}) copy-start(bf16[256,256]{1,0:T(8,128)(2,1)} %constant.28.clone.table_ref) | copy-start | bytes 393220
  7.0 36.6 %copy-start.4 = (f32[1,1,28672]{2,1,0:T(1,128)S(1)}, f32[1,1,28672]{2,1,0:T(1,128)}, u32[]{:S(2)}) copy-start(f32[1,1,28672]{2,1,0:T(1,128)} %param.7) | copy-start | bytes 344068
  7.1 58.0 %copy-start.2 = (bf16[256,256]{1,0:T(8,128)(2,1)S(1)}, bf16[256,256]{1,0:T(8,128)(2,1)}, u32[]{:S(2)}) copy-start(bf16[256,256]{1,0:T(8,128)(2,1)} %constant.29.clone.table_ref) | copy-start | bytes 393220
  7.1 58.0 %copy-start.5 = (bf16[256,128]{1,0:T(8,128)(2,1)S(1)}, bf16[256,128]{1,0:T(8,128)(2,1)}, u32[]{:S(2)}) copy-start(bf16[256,128]{1,0:T(8,128)(2,1)} %constant.30.clone.ones_ref) | copy-start | bytes 196612

commit v5 on v4

--- a/solution.py
+++ b/solution.py
@@ -62,42 +62,35 @@
     return lax.dot_general(parts, ones_ref[...], (((0,), (0,)), ((), ())), preferred_element_type=f32)
 
 
-def same_core_rows(x, odd):
-    upper, lower = x[:8], x[8:]
-    row = lax.broadcasted_iota(jnp.int32, upper.shape, 0)
-    even_place = row % 2 == 0
-    return jnp.where(
-        odd,
-        jnp.where(even_place, pltpu.roll(upper, 7, 0), lower),
-        jnp.where(even_place, upper, pltpu.roll(lower, 1, 0)),
-    )
-
-
-def pack_kernel(other, odd_ref, grad_ref, out_ref):
-    odd = (odd_ref[0] != 0) != other
-    for first in range(0, out_ref.shape[1], 8):
-        mixed = jnp.stack(
-            [
-                same_core_rows(grad_ref[:, tile * lanes : (tile + 1) * lanes], odd)
-                for tile in range(first, first + 8)
-            ]
+def pack_kernel(other, core_ref, grad_ref, out_ref, done):
+    core = 1 - core_ref[0] if other else core_ref[0]
+    places = grad_ref.shape[2] // 2
+    copies = [
+        pltpu.make_async_copy(
+            grad_ref.at[z // places, :, 2 * (z % places) + core, :], out_ref.at[z], done.at[z]
         )
-        rows = jnp.swapaxes(mixed, 0, 1)
-        for place in range(8):
-            out_ref[place // 2 + 4 * (place % 2), first : first + 8, :] = rows[place]
-
-
-def pack(grad, odd, other):
+        for z in range(out_ref.shape[0])
+    ]
+    for copy in copies:
+        copy.start()
+    for copy in copies:
+        copy.wait()
+
+
+def pack(grad, core, other):
     rows, columns = grad.shape
+    tiles = columns // lanes
+    grouped = grad.reshape(rows // 8, 8, tiles, lanes).transpose(0, 2, 1, 3)
     return pl.pallas_call(
         functools.partial(pack_kernel, other),
-        in_specs=[smem, whole],
+        in_specs=[smem, pl.BlockSpec(memory_space=pl.ANY)],
         out_specs=whole,
-        out_shape=jax.ShapeDtypeStruct((rows // 2, columns // lanes, lanes), f32),
-        compiler_params=params,
-        cost_estimate=pl.CostEstimate(flops=rows * columns, bytes_accessed=6 * rows * columns, transcendentals=0),
+        out_shape=jax.ShapeDtypeStruct((rows // 2, tiles, lanes), f32),
+        scratch_shapes=[pltpu.SemaphoreType.DMA((rows // 2,))],
+        compiler_params=pltpu.CompilerParams(vmem_limit_bytes=52 * 2**20),
+        cost_estimate=pl.CostEstimate(flops=0, bytes_accessed=4 * rows * columns, transcendentals=0),
         name="pack_other" if other else "pack_own",
-    )(odd, grad)
+    )(core, grouped)
 
 
 def places_kernel(places_ref, out_ref):
@@ -166,23 +159,36 @@
     return dense
 
 
-def outputs_kernel(me_ref, kept_ref, places_ref, accumulated_ref, table_ref, ones_ref, update_ref, moment_ref):
+def outputs_kernel(me_ref, kept_ref, places_ref, accumulated_ref, table_ref, ones_ref, update_ref, moment_ref, update, moment, done):
     replicas, _, half = kept_ref.shape
+    copies = []
+
+    def send(source, target, at):
+        copies.append(pltpu.make_async_copy(source.at[at], target.at[at], done.at[len(copies)]))
+        copies[-1].start()
+
+    own = []
+    level = lax.broadcasted_iota(jnp.int32, (block, half), 0).astype(f32)
+    for parity in range(2):
+        own.append(dense_of(kept_ref, places_ref, me_ref[0], parity, slice(0, half), level))
+    moment[...] = accumulated_ref[...] - inverse(jnp.concatenate(own, axis=0), table_ref)
+    send(moment, moment_ref, slice(0, half))
     for first in range(0, half, lanes):
         at = slice(first, min(first + lanes, half))
         level = lax.broadcasted_iota(jnp.int32, (block, at.stop - first), 0).astype(f32)
-        own, sums = [], []
+        sums = []
         for parity in range(2):
-            own.append(dense_of(kept_ref, places_ref, me_ref[0], parity, at, level))
             total = jnp.zeros(level.shape, f32)
             for replica in range(replicas):
                 total = total + dense_of(kept_ref, places_ref, replica, parity, at, level)
             sums.append(total * (1.0 / replicas))
-        moment_ref[at, :] = accumulated_ref[at, :] - inverse(jnp.concatenate(own, axis=0), table_ref)
         mean = jnp.concatenate(sums, axis=0)
         averaged = inverse(mean, table_ref)
         meansq = block_sums(mean * mean, ones_ref) * (1.0 / block)
-        update_ref[at, :] = averaged * lax.rsqrt(averaged * averaged + meansq + epsilon)
+        update[at, :] = averaged * lax.rsqrt(averaged * averaged + meansq + epsilon)
+        send(update, update_ref, at)
+    for copy in copies:
+        copy.wait()
 
 
 def outputs_step(me, kept, places, accumulated, table, ones):
@@ -190,8 +196,13 @@
     return pl.pallas_call(
         outputs_kernel,
         in_specs=[smem] + [whole] * 5,
-        out_specs=[whole, whole],
+        out_specs=[pl.BlockSpec(memory_space=pl.ANY)] * 2,
         out_shape=[jax.ShapeDtypeStruct(accumulated.shape, f32)] * 2,
+        scratch_shapes=[
+            pltpu.VMEM(accumulated.shape, f32),
+            pltpu.VMEM(accumulated.shape, f32),
+            pltpu.SemaphoreType.DMA((1 + pl.cdiv(half, lanes),)),
+        ],
         compiler_params=params,
         cost_estimate=pl.CostEstimate(flops=9 * replicas * lanes * half, bytes_accessed=8 * kept.size, transcendentals=lanes * half),
         name="outputs_step",
@@ -203,13 +214,13 @@
     tiles = columns // lanes
     devices = lax.axis_size("fsdp")
     me = lax.axis_index("fsdp")
-    odd = (me % 2).reshape(1)
+    core = (me % 2).reshape(1)
     grad = grad_parts[0, 0]
     forward_table, inverse_table, ones = (jnp.asarray(table) for table in tables())
     replica = lax.axis_index("dp").reshape(1)
-    sent = pack(grad, odd, True)
+    sent = pack(grad, core, True)
     arrived = lax.ppermute(sent, "fsdp", [(i, i ^ 1) for i in range(devices)])
-    own = pack(grad, odd, False)
+    own = pack(grad, core, False)
     places = split_places(positions[:, 0])
     own, places, arrived, replica = lax.optimization_barrier((own, places, arrived, replica))
     groups = [list(range(core, devices, 2)) for core in range(2)]

time: 67.5 us -> 67 us (level)
  Pallas kernels: 3.34 us -> 5.35 us
  local copies, waits for them, and re-layouts: 1.52 us -> 0.03 us
  waiting for transfers between devices: 1.86 us -> 0.85 us
    pallas_call x2, Pallas kernels: 0.6 us -> 2.65 us  [pack(): pl.pallas_call(functools.partial(pack_kernel, other), in_specs=[smem, pl....]
    unnamed x12 -> x10, local copies, waits for them, and re-layouts: 1.52 us -> 0.03 us
    ppermute x1, waiting for transfers between devices: 1.86 us -> 0.85 us  [body(): arrived = lax.ppermute(sent, 'fsdp', [(i, i ^ 1) for i in range(devices)])]
  transfers between devices with their start and end apart: 1 -> 1, of which waited for: 1 -> 1; matrix products, arithmetic and copies ran while one was open for 0% -> 0% of each run, Pallas kernels for 1% -> 2%
where the time goes in v5:
time: 67 us; the launch traced here: 66.7 us
  blocking collectives  57.6 us (86%)
  Pallas kernels  5.35 us (8%)
  starting transfers between devices  2.05 us (3%)
  waiting for transfers between devices  0.85 us (1%)
  between operations  0.72 us (1%)
    all_to_all x1, blocking collectives, body(): lax.all_to_all(own + arrived, 'fsdp', 0, 0, tiled=True, axis_index_groups...  36.5 us
    all_to_all x1, blocking collectives, body(): everyone = lax.all_to_all(copies, 'dp', 0, 0, tiled=True)  21.2 us
    pallas_call x2, Pallas kernels, pack(): pl.pallas_call(functools.partial(pack_kernel, other), in_specs=[smem, pl....  2.65 us
    pallas_call x1, Pallas kernels, outputs_step(): pl.pallas_call(outputs_kernel, in_specs=[smem] + [whole] * 5, out_specs=[...  2.17 us
    ppermute x1, starting transfers between devices, body(): arrived = lax.ppermute(sent, 'fsdp', [(i, i ^ 1) for i in range(devices)])  2.05 us
  transfers between devices with their start and end apart: 1, of which 1 were waited for; matrix products, arithmetic and copies ran while one was open for 0% of the time, Pallas kernels for 2%

profile of v5, /device:TPU:8, one launch (start us, length us, event | category | flops | bytes accessed | tf_op | source)
XLA Modules:
  0.0 66.7 jit_solution(10077976821017301956)
XLA Ops:
  0.6 1.3 %pack_other.1 = f32[8,224,128]{2,1,0:T(8,128)S(1)} custom-call(s32[1]{0:T(128)} %bitcast.core_ref, f32[2,224,8,128]{3,2,1,0:T(8,128)} %bitcast.11), custom_call_target="tpu_custom_call" | custom-call | bytes 1835008 | tf_op jit(solution)/shard_map/pack_other/pallas_call | solution.py:84
  2.0 0.0 copy-start
  2.0 2.1 %collective-permute-start = (f32[8,224,128]{2,1,0:T(8,128)S(1)}, f32[8,224,128]{2,1,0:T(8,128)S(1)}, u32[]{:S(2)}, u32[]{:S(2)}) collective-permute-start(f32[8,224,128]{2,1,0:T(8,128)S(1)} %pack_other.1), channel_id=1, source_target_pairs={{0,1},{1,0},{2,3},{3,2},{4,5},{5,4},{6,7},{7,6},{8,9},{9,8},{10,11... | collective-permute-start | bytes 2752520 | tf_op jit(solution)/shard_map/ppermute | solution.py:222
  4.0 1.3 %pack_own.1 = f32[8,224,128]{2,1,0:T(8,128)S(1)} custom-call(s32[1]{0:T(128)} %bitcast.core_ref, f32[2,224,8,128]{3,2,1,0:T(8,128)} %bitcast.12), custom_call_target="tpu_custom_call" | custom-call | bytes 1835008 | tf_op jit(solution)/shard_map/pack_own/pallas_call | solution.py:84
  5.4 0.0 copy-done
  5.4 0.2 split_places.1.places_ref
  5.6 0.8 %collective-permute-done = f32[8,224,128]{2,1,0:T(8,128)S(1)} collective-permute-done((f32[8,224,128]{2,1,0:T(8,128)S(1)}, f32[8,224,128]{2,1,0:T(8,128)S(1)}, u32[]{:S(2)}, u32[]{:S(2)}) %collective-permute-start) | collective-permute-done | bytes 917536 | tf_op jit(solution)/shard_map/ppermute | solution.py:222
  6.5 0.0 copy-start.2
  6.5 0.0 copy-start.3
  6.5 0.1 add.8
  6.6 0.0 copy-start.1
  6.6 0.0 copy-start.4
  6.6 36.5 %all_to_all.10.parts_ref = f32[8,224,128]{2,1,0:T(8,128)S(1)} all-to-all(f32[8,224,128]{2,1,0:T(8,128)S(1)} %add.8), channel_id=1, replica_groups={{0,2,4,6,8,10,12,14},{1,3,5,7,9,11,13,15},{16,18,20,22,24,26,28,30},{17..., dimensions={0} | all-to-all | bytes 1835008 | tf_op jit(solution)/shard_map/all_to_all | solution.py:227
  43.1 0.0 copy-done.2
  43.1 0.0 copy-done.3
  43.1 0.3 kept_step.1
  43.4 21.2 %all_to_all.11.kept_ref = f32[32,8,224]{2,1,0:T(8,128)S(1)} all-to-all(f32[32,8,224]{2,1,0:T(8,128)S(1)} %get-tuple-element.14), channel_id=1, replica_groups=mesh['dp'=32,'fsdp'=16] {'dp'}, dimensions={0} | all-to-all | bytes 458752 | tf_op jit(solution)/shard_map/all_to_all | solution.py:229
  64.5 0.0 copy-done.1
  64.6 0.0 copy-done.4
  64.6 2.2 %outputs_step.1 = (f32[224,128]{1,0:T(8,128)}, f32[224,128]{1,0:T(8,128)}) custom-call(s32[1]{0:T(128)} %bitcast.5.me_ref, f32[32,8,224]{2,1,0:T(8,128)S(1)} %all_to_all.11.kept_ref, f32[32,8,224]{2,1,0:T(8,128)S(1)} %split_places.1.places_ref, f32[224,128]{1,0:T(8,128)S(1)} %get-tuple-element.15.accumulated_ref, bf16[256,256]{1,0:T(8,128)(2,1)S(1)} %copy-done.1, ...), custom_call_target="tpu_custom_call" | custom-call | flops 8257536 | bytes 458752 | tf_op jit(solution)/shard_map/outputs_step/pallas_call | solution.py:196
Async XLA Ops:
  2.0 3.4 %copy-start = (s32[32,1,4,448]{3,2,1,0:T(4,128)S(1)}, s32[32,1,4,448]{3,2,1,0:T(4,128)}, u32[]{:S(2)}) copy-start(s32[32,1,4,448]{3,2,1,0:T(4,128)} %param.8) | copy-start | bytes 688132
  2.0 4.5 %collective-permute-start = (f32[8,224,128]{2,1,0:T(8,128)S(1)}, f32[8,224,128]{2,1,0:T(8,128)S(1)}, u32[]{:S(2)}, u32[]{:S(2)}) collective-permute-start(f32[8,224,128]{2,1,0:T(8,128)S(1)} %pack_other.1), channel_id=1, source_target_pairs={{0,1},{1,0},{2,3},{3,2},{4,5},{5,4},{6,7},{7,6},{8,9},{9,8},{10,11... | collective-permute-start | bytes 2752520 | tf_op jit(solution)/shard_map/ppermute | solution.py:222
  6.5 36.6 %copy-start.2 = (bf16[256,256]{1,0:T(8,128)(2,1)S(1)}, bf16[256,256]{1,0:T(8,128)(2,1)}, u32[]{:S(2)}) copy-start(bf16[256,256]{1,0:T(8,128)(2,1)} %constant.28.clone.table_ref) | copy-start | bytes 393220
  6.5 36.6 %copy-start.3 = (f32[1,1,28672]{2,1,0:T(1,128)S(1)}, f32[1,1,28672]{2,1,0:T(1,128)}, u32[]{:S(2)}) copy-start(f32[1,1,28672]{2,1,0:T(1,128)} %param.7) | copy-start | bytes 344068
  6.6 58.0 %copy-start.1 = (bf16[256,256]{1,0:T(8,128)(2,1)S(1)}, bf16[256,256]{1,0:T(8,128)(2,1)}, u32[]{:S(2)}) copy-start(bf16[256,256]{1,0:T(8,128)(2,1)} %constant.29.clone.table_ref) | copy-start | bytes 393220
  6.6 58.0 %copy-start.4 = (bf16[256,128]{1,0:T(8,128)(2,1)S(1)}, bf16[256,128]{1,0:T(8,128)(2,1)}, u32[]{:S(2)}) copy-start(bf16[256,128]{1,0:T(8,128)(2,1)} %constant.30.clone.ones_ref) | copy-start | bytes 196612

commit v6 on v5

v6 whole, which is shorter than its diff:
```python
import functools

import jax
import jax.numpy as jnp
import numpy as np
from jax import lax
from jax.experimental import pallas as pl
from jax.experimental.pallas import tpu as pltpu
from jax.sharding import PartitionSpec as P

decay_rate = 0.999
epsilon = 1e-06
block = 64
lanes = 128
keep = 4
f32, bf16 = jnp.float32, jnp.bfloat16
whole = pl.BlockSpec(memory_space=pltpu.VMEM)
smem = pl.BlockSpec(memory_space=pltpu.SMEM)
anywhere = pl.BlockSpec(memory_space=pl.ANY)
params = pltpu.CompilerParams(vmem_limit_bytes=12 * 2**20)
narrow = pltpu.CompilerParams(vmem_limit_bytes=51 * 2**20)


def paired_table():
    frequency = np.arange(block)[:, None]
    sample = np.arange(block)[None, :]
    cosines = np.cos(np.pi * (2.0 * sample + 1.0) * frequency / (2.0 * block))
    norming = np.where(frequency == 0, np.sqrt(1.0 / block), np.sqrt(2.0 / block))
    return np.kron(np.eye(2), cosines * norming).astype(np.float32)


def tables():
    table = paired_table()
    high = table.astype(jnp.bfloat16)
    low = (table - high.astype(np.float32)).astype(jnp.bfloat16)
    none = np.zeros_like(high)
    return np.block([[high, high], [low, none]]), np.block([[high.T, high.T], [low.T, none]])


def halves(x):
    high = x.astype(bf16)
    return high, (x - high.astype(f32)).astype(bf16)


def forward(fields, table_ref):
    parts = jnp.concatenate(halves(fields), axis=1)
    both = lax.dot_general(table_ref[...], parts, (((1,), (1,)), ((), ())), preferred_element_type=f32)
    return both[:lanes] + both[lanes:]


def inverse(coeffs, table_ref):
    parts = jnp.concatenate(halves(coeffs), axis=0)
    both = jnp.dot(table_ref[...], parts, preferred_element_type=f32)
    return both[:lanes] + both[lanes:]


def row_copies(core, grad_ref, out_ref, done):
    places = grad_ref.shape[2] // 2
    return [
        pltpu.make_async_copy(
            grad_ref.at[z // places, :, 2 * (z % places) + core, :], out_ref.at[z], done.at[z]
        )
        for z in range(out_ref.shape[0])
    ]


def pack_kernel(core_ref, grad_ref, out_ref, done):
    copies = row_copies(1 - core_ref[0], grad_ref, out_ref, done)
    for copy in copies:
        copy.start()
    for copy in copies:
        copy.wait()


def pack_other(grouped, core):
    groups, tiles, places, _ = grouped.shape
    rows = groups * places // 2
    return pl.pallas_call(
        pack_kernel,
        in_specs=[smem, anywhere],
        out_specs=whole,
        out_shape=jax.ShapeDtypeStruct((rows, tiles, lanes), f32),
        scratch_shapes=[pltpu.SemaphoreType.DMA((rows,))],
        compiler_params=pltpu.CompilerParams(vmem_limit_bytes=52 * 2**20),
        cost_estimate=pl.CostEstimate(flops=0, bytes_accessed=4 * grouped.size, transcendentals=0),
        name="pack_other",
    )(core, grouped)


def prepare_kernel(core_ref, me_ref, grad_ref, places_ref, own_ref, index_ref, mine_ref, split, done):
    copies = row_copies(core_ref[0], grad_ref, own_ref, done)
    for copy in copies:
        copy.start()
    replicas, count, spans = places_ref.shape
    half = spans // 2
    source = lax.broadcasted_iota(jnp.int32, (spans, half), 0)
    target = lax.broadcasted_iota(jnp.int32, (spans, half), 1)
    places = places_ref[...].reshape(replicas * count, spans).astype(f32).astype(bf16)
    for parity in range(2):
        chooser = (source == 2 * target + parity).astype(f32).astype(bf16)
        chosen = jnp.dot(places, chooser, preferred_element_type=f32)
        split[:, parity * count : (parity + 1) * count, :] = chosen.reshape(replicas, count, half)
    mine_ref[...] = split[me_ref[0]]
    level = lax.broadcasted_iota(jnp.int32, (block, half), 0).astype(f32)
    for parity in range(2):
        nothing = count * (1 - parity)
        for word in range(replicas // 8):
            packed = jnp.zeros(level.shape, jnp.int32)
            for field in range(8):
                row_of = jnp.full(level.shape, nothing << (4 * field), jnp.int32)
                for j in range(count):
                    row = parity * count + j
                    here = split[word * 8 + field, row : row + 1, :] == level
                    row_of = jnp.where(here, row << (4 * field), row_of)
                packed = packed | row_of
            index_ref[word, parity * block : (parity + 1) * block, :] = packed
    for copy in copies:
        copy.wait()


def prepare(core, me, grouped, positions):
    groups, tiles, places, _ = grouped.shape
    rows = groups * places // 2
    replicas, count, spans = positions.shape
    half = spans // 2
    return pl.pallas_call(
        prepare_kernel,
        in_specs=[smem, smem, anywhere, whole],
        out_specs=[whole] * 3,
        out_shape=[
            jax.ShapeDtypeStruct((rows, tiles, lanes), f32),
            jax.ShapeDtypeStruct((replicas // 8, 2 * block, half), jnp.int32),
            jax.ShapeDtypeStruct((2 * count, half), f32),
        ],
        scratch_shapes=[
            pltpu.VMEM((replicas, 2 * count, half), f32),
            pltpu.SemaphoreType.DMA((rows,)),
        ],
        compiler_params=narrow,
        cost_estimate=pl.CostEstimate(flops=9 * replicas * lanes * half, bytes_accessed=4 * grouped.size, transcendentals=0),
        name="prepare",
    )(core, me, grouped, positions)


def kept_kernel(parts_ref, moment_ref, places_ref, table_ref, copies_ref, accumulated_ref):
    gradient = parts_ref[0]
    for source in range(1, parts_ref.shape[0]):
        gradient = gradient + parts_ref[source]
    accumulated = decay_rate * moment_ref[...] + gradient
    accumulated_ref[...] = accumulated
    coeffs = forward(accumulated, table_ref)
    level = lax.broadcasted_iota(jnp.int32, (block, coeffs.shape[1]), 0).astype(f32)
    own = places_ref[...]
    kept = []
    for parity in range(2):
        mine = coeffs[parity * block : (parity + 1) * block]
        for j in range(keep):
            row = parity * keep + j
            kept.append(jnp.sum(jnp.where(own[row : row + 1] == level, mine, 0.0), axis=0, keepdims=True))
    copies_ref[...] = jnp.broadcast_to(jnp.concatenate(kept, axis=0)[None], copies_ref.shape)


def kept_step(parts, moment, places, table, replicas):
    return pl.pallas_call(
        kept_kernel,
        in_specs=[whole] * 4,
        out_specs=[whole, whole],
        out_shape=[
            jax.ShapeDtypeStruct((replicas,) + places.shape, f32),
            jax.ShapeDtypeStruct(moment.shape, f32),
        ],
        compiler_params=params,
        cost_estimate=pl.CostEstimate(flops=6 * moment.size * lanes, bytes_accessed=4 * parts.size, transcendentals=0),
        name="kept_step",
    )(parts, moment, places, table)


def by_parity(values):
    even = lax.broadcasted_iota(jnp.int32, values.shape, 0) < keep
    return jnp.where(even, values, 0.0), jnp.where(even, 0.0, values)


def placed(values, word, shift):
    rows = lax.shift_right_logical(word, jnp.full(word.shape, shift, jnp.int32)) & 7
    return jnp.take_along_axis(values, rows, axis=0, mode="promise_in_bounds")


def outputs_kernel(me_ref, kept_ref, index_ref, accumulated_ref, table_ref, update_ref, moment_ref, update, moment, done):
    replicas, _, half = kept_ref.shape
    chunks = range(0, 2 * block, 8)
    copies = []

    def send(source, target, at):
        copies.append(pltpu.make_async_copy(source.at[at], target.at[at], done.at[len(copies)]))
        copies[-1].start()

    me = me_ref[0]
    sides = by_parity(kept_ref[me])
    own = [placed(sides[k // block], index_ref[me // 8, k : k + 8, :], me % 8 * 4) for k in chunks]
    moment[...] = accumulated_ref[...] - inverse(jnp.concatenate(own, axis=0), table_ref).T
    send(moment, moment_ref, slice(0, half))
    for first in range(0, half, lanes):
        at = slice(first, min(first + lanes, half))
        sums = [jnp.zeros((8, at.stop - first), f32) for _ in chunks]
        for replica in range(replicas):
            sides = by_parity(kept_ref[replica, :, at])
            sums = [
                total + placed(sides[k // block], index_ref[replica // 8, k : k + 8, at], replica % 8 * 4)
                for k, total in zip(chunks, sums)
            ]
        mean = jnp.concatenate(sums, axis=0) * (1.0 / replicas)
        averaged = inverse(mean, table_ref)
        parts = []
        for side in (slice(0, block), slice(block, 2 * block)):
            meansq = jnp.sum(mean[side] * mean[side], axis=0, keepdims=True) * (1.0 / block)
            parts.append(averaged[side] * lax.rsqrt(averaged[side] * averaged[side] + (meansq + epsilon)))
        update[at, :] = jnp.concatenate(parts, axis=0).T
        send(update, update_ref, at)
    for copy in copies:
        copy.wait()


def outputs_step(me, kept, index, accumulated, table):
    replicas, _, half = kept.shape
    return pl.pallas_call(
        outputs_kernel,
        in_specs=[smem] + [whole] * 4,
        out_specs=[anywhere] * 2,
        out_shape=[jax.ShapeDtypeStruct(accumulated.shape, f32)] * 2,
        scratch_shapes=[
            pltpu.VMEM(accumulated.shape, f32),
            pltpu.VMEM(accumulated.shape, f32),
            pltpu.SemaphoreType.DMA((1 + pl.cdiv(half, lanes),)),
        ],
        compiler_params=params,
        cost_estimate=pl.CostEstimate(flops=9 * replicas * lanes * half, bytes_accessed=8 * kept.size, transcendentals=lanes * half),
        name="outputs_step",
    )(me, kept, index, accumulated, table)


def body(grad_parts, momentum, positions):
    columns = momentum.shape[-1]
    tiles = columns // lanes
    devices = lax.axis_size("fsdp")
    me = lax.axis_index("fsdp")
    core = (me % 2).reshape(1)
    rows = grad_parts.shape[2]
    grouped = grad_parts[0, 0].reshape(rows // 8, 8, tiles, lanes).transpose(0, 2, 1, 3)
    positions = positions[:, 0]
    forward_table, inverse_table = (jnp.asarray(table) for table in tables())
    replica = lax.axis_index("dp").reshape(1)
    arrived = lax.ppermute(pack_other(grouped, core), "fsdp", [(i, i ^ 1) for i in range(devices)])
    own, index, places = prepare(core, replica, grouped, positions)
    own, index, places, arrived, replica = lax.optimization_barrier((own, index, places, arrived, replica))
    groups = [list(range(side, devices, 2)) for side in range(2)]
    parts = lax.all_to_all(own + arrived, "fsdp", 0, 0, tiled=True, axis_index_groups=groups)
    copies, accumulated = kept_step(parts, momentum.reshape(tiles, lanes), places, forward_table, positions.shape[0])
    everyone = lax.all_to_all(copies, "dp", 0, 0, tiled=True)
    update, new_moment = outputs_step(replica, everyone, index, accumulated, inverse_table)
    return update.reshape(1, columns), new_moment.reshape(1, 1, columns)


def solution(mesh):
    in_specs = (P("dp", "fsdp", None, None), P("dp", "fsdp", None), P(None, "fsdp", None, None))
    out_specs = (P("fsdp", None), P("dp", "fsdp", None))
    return jax.shard_map(body, mesh=mesh, in_specs=in_specs, out_specs=out_specs, check_vma=False)
```

time: 67 us -> 66.8 us (level)
    pallas_call x5 -> x4, Pallas kernels: 5.35 us -> 5.36 us  [the longest x1 2.07 us: outputs_step(): pl.pallas_call(outputs_kernel, in_specs=[smem] + [whole] * 4, out_specs=[...]
where the time goes in v6:
time: 66.8 us; the launch traced here: 66.5 us
  blocking collectives  57.6 us (86%)
  Pallas kernels  5.36 us (8%)
  starting transfers between devices  1.92 us (3%)
  waiting for transfers between devices  0.78 us (1%)
  between operations  0.71 us (1%)
    all_to_all x1, blocking collectives, body(): lax.all_to_all(own + arrived, 'fsdp', 0, 0, tiled=True, axis_index_groups...  36.5 us
    all_to_all x1, blocking collectives, body(): everyone = lax.all_to_all(copies, 'dp', 0, 0, tiled=True)  21.2 us
    pallas_call x1, Pallas kernels, outputs_step(): pl.pallas_call(outputs_kernel, in_specs=[smem] + [whole] * 4, out_specs=[...  2.07 us
    ppermute x1, starting transfers between devices, body(): lax.ppermute(pack_other(grouped, core), 'fsdp', [(i, i ^ 1) for i in rang...  1.92 us
    pallas_call x1, Pallas kernels, prepare(): pl.pallas_call(prepare_kernel, in_specs=[smem, smem, anywhere, whole], ou...  1.64 us
    pallas_call x1, Pallas kernels, pack_other(): pl.pallas_call(pack_kernel, in_specs=[smem, anywhere], out_specs=whole, o...  1.35 us
  transfers between devices with their start and end apart: 1, of which 1 were waited for; matrix products, arithmetic and copies ran while one was open for 0% of the time, Pallas kernels for 2%

profile of v6, /device:TPU:8, one launch (start us, length us, event | category | flops | bytes accessed | tf_op | source)
XLA Modules:
  0.0 66.5 jit_solution(2356871005780045239)
XLA Ops:
  0.6 0.0 copy-start
  0.7 1.4 %pack_other.1 = f32[8,224,128]{2,1,0:T(8,128)S(1)} custom-call(s32[1]{0:T(128)} %bitcast.core_ref, f32[2,224,8,128]{3,2,1,0:T(8,128)} %bitcast.11), custom_call_target="tpu_custom_call" | custom-call | bytes 1835008 | tf_op jit(solution)/shard_map/pack_other/pallas_call | solution.py:78
  2.0 1.9 %collective-permute-start = (f32[8,224,128]{2,1,0:T(8,128)S(1)}, f32[8,224,128]{2,1,0:T(8,128)S(1)}, u32[]{:S(2)}, u32[]{:S(2)}) collective-permute-start(f32[8,224,128]{2,1,0:T(8,128)S(1)} %pack_other.1), channel_id=1, source_target_pairs={{0,1},{1,0},{2,3},{3,2},{4,5},{5,4},{6,7},{7,6},{8,9},{9,8},{10,11... | collective-permute-start | bytes 2752520 | tf_op jit(solution)/shard_map/ppermute | solution.py:252
  3.9 0.0 copy-done
  4.0 1.6 %prepare.1 = (f32[8,224,128]{2,1,0:T(8,128)S(1)}, s32[4,128,224]{2,1,0:T(8,128)S(1)}, f32[8,224]{1,0:T(8,128)S(1)}) custom-call(s32[1]{0:T(128)} %bitcast.core_ref, s32[1]{0:T(128)} %bitcast.1.me_ref, f32[2,224,8,128]{3,2,1,0:T(8,128)} %bitcast.12, s32[32,4,448]{2,1,0:T(4,128)S(1)} %bitcast.9), custom_call_target="tpu_custom_call" | custom-call | flops 8257536 | bytes 1835008 | tf_op jit(solution)/shard_map/prepare/pallas_call | solution.py:126
  5.6 0.8 %collective-permute-done = f32[8,224,128]{2,1,0:T(8,128)S(1)} collective-permute-done((f32[8,224,128]{2,1,0:T(8,128)S(1)}, f32[8,224,128]{2,1,0:T(8,128)S(1)}, u32[]{:S(2)}, u32[]{:S(2)}) %collective-permute-start) | collective-permute-done | bytes 917536 | tf_op jit(solution)/shard_map/ppermute | solution.py:252
  6.4 0.0 copy-start.2
  6.4 0.0 copy-start.3
  6.4 0.1 add.8
  6.5 0.0 copy-start.1
  6.5 36.5 %all_to_all.10.parts_ref = f32[8,224,128]{2,1,0:T(8,128)S(1)} all-to-all(f32[8,224,128]{2,1,0:T(8,128)S(1)} %add.8), channel_id=1, replica_groups={{0,2,4,6,8,10,12,14},{1,3,5,7,9,11,13,15},{16,18,20,22,24,26,28,30},{17..., dimensions={0} | all-to-all | bytes 1835008 | tf_op jit(solution)/shard_map/all_to_all | solution.py:256
  43.0 0.0 copy-done.2
  43.0 0.0 copy-done.3
  43.0 0.3 kept_step.1
  43.3 21.2 %all_to_all.11.kept_ref = f32[32,8,224]{2,1,0:T(8,128)S(1)} all-to-all(f32[32,8,224]{2,1,0:T(8,128)S(1)} %get-tuple-element.21), channel_id=1, replica_groups=mesh['dp'=32,'fsdp'=16] {'dp'}, dimensions={0} | all-to-all | bytes 458752 | tf_op jit(solution)/shard_map/all_to_all | solution.py:258
  64.5 0.0 copy-done.1
  64.5 2.1 %outputs_step.1 = (f32[224,128]{1,0:T(8,128)}, f32[224,128]{1,0:T(8,128)}) custom-call(s32[1]{0:T(128)} %bitcast.1.me_ref, f32[32,8,224]{2,1,0:T(8,128)S(1)} %all_to_all.11.kept_ref, s32[4,128,224]{2,1,0:T(8,128)S(1)} %get-tuple-element.22.index_ref, f32[224,128]{1,0:T(8,128)S(1)} %get-tuple-element.23.accumulated_ref, bf16[256,256]{1,0:T(8,128)(2,1)S(1)} %copy-done.1), custom_call_target="tpu_custom_call" | custom-call | flops 8257536 | bytes 458752 | tf_op jit(solution)/shard_map/outputs_step/pallas_call | solution.py:225
Async XLA Ops:
  0.6 3.3 %copy-start = (s32[32,1,4,448]{3,2,1,0:T(4,128)S(1)}, s32[32,1,4,448]{3,2,1,0:T(4,128)}, u32[]{:S(2)}) copy-start(s32[32,1,4,448]{3,2,1,0:T(4,128)} %param.7) | copy-start | bytes 688132
  2.0 4.4 %collective-permute-start = (f32[8,224,128]{2,1,0:T(8,128)S(1)}, f32[8,224,128]{2,1,0:T(8,128)S(1)}, u32[]{:S(2)}, u32[]{:S(2)}) collective-permute-start(f32[8,224,128]{2,1,0:T(8,128)S(1)} %pack_other.1), channel_id=1, source_target_pairs={{0,1},{1,0},{2,3},{3,2},{4,5},{5,4},{6,7},{7,6},{8,9},{9,8},{10,11... | collective-permute-start | bytes 2752520 | tf_op jit(solution)/shard_map/ppermute | solution.py:252
  6.4 36.6 %copy-start.2 = (bf16[256,256]{1,0:T(8,128)(2,1)S(1)}, bf16[256,256]{1,0:T(8,128)(2,1)}, u32[]{:S(2)}) copy-start(bf16[256,256]{1,0:T(8,128)(2,1)} %constant.26.clone.table_ref) | copy-start | bytes 393220
  6.4 36.6 %copy-start.3 = (f32[1,1,28672]{2,1,0:T(1,128)S(1)}, f32[1,1,28672]{2,1,0:T(1,128)}, u32[]{:S(2)}) copy-start(f32[1,1,28672]{2,1,0:T(1,128)} %param.6) | copy-start | bytes 344068
  6.5 58.0 %copy-start.1 = (bf16[256,256]{1,0:T(8,128)(2,1)S(1)}, bf16[256,256]{1,0:T(8,128)(2,1)}, u32[]{:S(2)}) copy-start(bf16[256,256]{1,0:T(8,128)(2,1)} %constant.27.clone.table_ref) | copy-start | bytes 393220

commit v7 on v6

--- a/solution.py
+++ b/solution.py
@@ -21,6 +21,16 @@
 narrow = pltpu.CompilerParams(vmem_limit_bytes=51 * 2**20)
 
 
+def z_order(count):
+    return list(range(count - 1, -1, -1))
+
+
+def dp_order():
+    lag_x, lag_y = (0, 6, 9, 13), (0, 4, 12, 18, 31, 26, 24, 23)
+    lag = [x + y for x in lag_x for y in lag_y]
+    return sorted(range(len(lag)), key=lambda replica: (lag[replica], replica), reverse=True)
+
+
 def paired_table():
     frequency = np.arange(block)[:, None]
     sample = np.arange(block)[None, :]
@@ -87,7 +97,7 @@
     )(core, grouped)
 
 
-def prepare_kernel(core_ref, me_ref, grad_ref, places_ref, own_ref, index_ref, mine_ref, split, done):
+def prepare_kernel(core_ref, me_ref, grad_ref, places_ref, own_ref, index_ref, mine_ref, rows_ref, split, done):
     copies = row_copies(core_ref[0], grad_ref, own_ref, done)
     for copy in copies:
         copy.start()
@@ -102,18 +112,24 @@
         split[:, parity * count : (parity + 1) * count, :] = chosen.reshape(replicas, count, half)
     mine_ref[...] = split[me_ref[0]]
     level = lax.broadcasted_iota(jnp.int32, (block, half), 0).astype(f32)
+    order = dp_order()
+
+    def row_of(places, parity, shift):
+        rows = jnp.full(level.shape, (count * (1 - parity)) << shift, jnp.int32)
+        for j in range(count):
+            row = parity * count + j
+            rows = jnp.where(places(row) == level, row << shift, rows)
+        return rows
+
     for parity in range(2):
-        nothing = count * (1 - parity)
+        at = slice(parity * block, (parity + 1) * block)
+        rows_ref[at, :] = row_of(lambda row: mine_ref[row : row + 1, :], parity, 0)
         for word in range(replicas // 8):
             packed = jnp.zeros(level.shape, jnp.int32)
             for field in range(8):
-                row_of = jnp.full(level.shape, nothing << (4 * field), jnp.int32)
-                for j in range(count):
-                    row = parity * count + j
-                    here = split[word * 8 + field, row : row + 1, :] == level
-                    row_of = jnp.where(here, row << (4 * field), row_of)
-                packed = packed | row_of
-            index_ref[word, parity * block : (parity + 1) * block, :] = packed
+                replica = order[word * 8 + field]
+                packed = packed | row_of(lambda row: split[replica, row : row + 1, :], parity, 4 * field)
+            index_ref[word, at, :] = packed
     for copy in copies:
         copy.wait()
 
@@ -126,11 +142,12 @@
     return pl.pallas_call(
         prepare_kernel,
         in_specs=[smem, smem, anywhere, whole],
-        out_specs=[whole] * 3,
+        out_specs=[whole] * 4,
         out_shape=[
             jax.ShapeDtypeStruct((rows, tiles, lanes), f32),
             jax.ShapeDtypeStruct((replicas // 8, 2 * block, half), jnp.int32),
             jax.ShapeDtypeStruct((2 * count, half), f32),
+            jax.ShapeDtypeStruct((2 * block, half), jnp.int32),
         ],
         scratch_shapes=[
             pltpu.VMEM((replicas, 2 * count, half), f32),
@@ -142,7 +159,24 @@
     )(core, me, grouped, positions)
 
 
-def kept_kernel(parts_ref, moment_ref, places_ref, table_ref, copies_ref, accumulated_ref):
+def add_kernel(own_ref, arrived_ref, out_ref):
+    for place, z in enumerate(z_order(out_ref.shape[0])):
+        out_ref[place] = own_ref[z] + arrived_ref[z]
+
+
+def add_step(own, arrived):
+    return pl.pallas_call(
+        add_kernel,
+        in_specs=[whole, whole],
+        out_specs=whole,
+        out_shape=jax.ShapeDtypeStruct(own.shape, f32),
+        compiler_params=params,
+        cost_estimate=pl.CostEstimate(flops=own.size, bytes_accessed=12 * own.size, transcendentals=0),
+        name="add_step",
+    )(own, arrived)
+
+
+def kept_kernel(parts_ref, moment_ref, places_ref, table_ref, copies_ref, own_ref, accumulated_ref):
     gradient = parts_ref[0]
     for source in range(1, parts_ref.shape[0]):
         gradient = gradient + parts_ref[source]
@@ -157,16 +191,18 @@
         for j in range(keep):
             row = parity * keep + j
             kept.append(jnp.sum(jnp.where(own[row : row + 1] == level, mine, 0.0), axis=0, keepdims=True))
-    copies_ref[...] = jnp.broadcast_to(jnp.concatenate(kept, axis=0)[None], copies_ref.shape)
+    own_ref[...] = jnp.concatenate(kept, axis=0)
+    copies_ref[...] = jnp.broadcast_to(own_ref[...][None], copies_ref.shape)
 
 
 def kept_step(parts, moment, places, table, replicas):
     return pl.pallas_call(
         kept_kernel,
         in_specs=[whole] * 4,
-        out_specs=[whole, whole],
+        out_specs=[whole] * 3,
         out_shape=[
             jax.ShapeDtypeStruct((replicas,) + places.shape, f32),
+            jax.ShapeDtypeStruct(places.shape, f32),
             jax.ShapeDtypeStruct(moment.shape, f32),
         ],
         compiler_params=params,
@@ -180,12 +216,16 @@
     return jnp.where(even, values, 0.0), jnp.where(even, 0.0, values)
 
 
+def taken(values, rows):
+    return jnp.take_along_axis(values, rows, axis=0, mode="promise_in_bounds")
+
+
 def placed(values, word, shift):
     rows = lax.shift_right_logical(word, jnp.full(word.shape, shift, jnp.int32)) & 7
-    return jnp.take_along_axis(values, rows, axis=0, mode="promise_in_bounds")
-
-
-def outputs_kernel(me_ref, kept_ref, index_ref, accumulated_ref, table_ref, update_ref, moment_ref, update, moment, done):
+    return taken(values, rows)
+
+
+def outputs_kernel(kept_ref, index_ref, own_ref, rows_ref, accumulated_ref, table_ref, update_ref, moment_ref, update, moment, done):
     replicas, _, half = kept_ref.shape
     chunks = range(0, 2 * block, 8)
     copies = []
@@ -194,9 +234,8 @@
         copies.append(pltpu.make_async_copy(source.at[at], target.at[at], done.at[len(copies)]))
         copies[-1].start()
 
-    me = me_ref[0]
-    sides = by_parity(kept_ref[me])
-    own = [placed(sides[k // block], index_ref[me // 8, k : k + 8, :], me % 8 * 4) for k in chunks]
+    sides = by_parity(own_ref[...])
+    own = [taken(sides[k // block], rows_ref[k : k + 8, :]) for k in chunks]
     moment[...] = accumulated_ref[...] - inverse(jnp.concatenate(own, axis=0), table_ref).T
     send(moment, moment_ref, slice(0, half))
     for first in range(0, half, lanes):
@@ -220,11 +259,11 @@
         copy.wait()
 
 
-def outputs_step(me, kept, index, accumulated, table):
+def outputs_step(kept, index, own, rows, accumulated, table):
     replicas, _, half = kept.shape
     return pl.pallas_call(
         outputs_kernel,
-        in_specs=[smem] + [whole] * 4,
+        in_specs=[whole] * 6,
         out_specs=[anywhere] * 2,
         out_shape=[jax.ShapeDtypeStruct(accumulated.shape, f32)] * 2,
         scratch_shapes=[
@@ -235,7 +274,7 @@
         compiler_params=params,
         cost_estimate=pl.CostEstimate(flops=9 * replicas * lanes * half, bytes_accessed=8 * kept.size, transcendentals=lanes * half),
         name="outputs_step",
-    )(me, kept, index, accumulated, table)
+    )(kept, index, own, rows, accumulated, table)
 
 
 def body(grad_parts, momentum, positions):
@@ -250,13 +289,13 @@
     forward_table, inverse_table = (jnp.asarray(table) for table in tables())
     replica = lax.axis_index("dp").reshape(1)
     arrived = lax.ppermute(pack_other(grouped, core), "fsdp", [(i, i ^ 1) for i in range(devices)])
-    own, index, places = prepare(core, replica, grouped, positions)
-    own, index, places, arrived, replica = lax.optimization_barrier((own, index, places, arrived, replica))
-    groups = [list(range(side, devices, 2)) for side in range(2)]
-    parts = lax.all_to_all(own + arrived, "fsdp", 0, 0, tiled=True, axis_index_groups=groups)
-    copies, accumulated = kept_step(parts, momentum.reshape(tiles, lanes), places, forward_table, positions.shape[0])
-    everyone = lax.all_to_all(copies, "dp", 0, 0, tiled=True)
-    update, new_moment = outputs_step(replica, everyone, index, accumulated, inverse_table)
+    own, index, places, rows = prepare(core, replica, grouped, positions)
+    own, index, places, rows, arrived = lax.optimization_barrier((own, index, places, rows, arrived))
+    groups = [[2 * z + side for z in z_order(devices // 2)] for side in range(2)]
+    parts = lax.all_to_all(add_step(own, arrived), "fsdp", 0, 0, tiled=True, axis_index_groups=groups)
+    copies, kept, accumulated = kept_step(parts, momentum.reshape(tiles, lanes), places, forward_table, positions.shape[0])
+    everyone = lax.all_to_all(copies, "dp", 0, 0, tiled=True, axis_index_groups=[dp_order()])
+    update, new_moment = outputs_step(everyone, index, kept, rows, accumulated, inverse_table)
     return update.reshape(1, columns), new_moment.reshape(1, 1, columns)
 
 

time: 66.8 us -> 60.2 us (0.901)
  blocking collectives: 57.6 us -> 51.1 us
    all_to_all x2, blocking collectives: 57.6 us -> 51.1 us  [the longest x1 33.6 us: body(): lax.all_to_all(add_step(own, arrived), 'fsdp', 0, 0, tiled=True, axis_ind...]
    pallas_call x2 -> x3, Pallas kernels: 2.37 us -> 2.46 us  [the longest x1 2.05 us: outputs_step(): pl.pallas_call(outputs_kernel, in_specs=[whole] * 6, out_specs=[anywhere]...]
  transfers between devices with their start and end apart: 1 -> 1, of which waited for: 1 -> 1; matrix products, arithmetic and copies ran while one was open for 0% -> 0% of each run, Pallas kernels for 2% -> 3%
where the time goes in v7:
time: 60.2 us; the launch traced here: 60 us
  blocking collectives  51.1 us (85%)
  Pallas kernels  5.67 us (9%)
  starting transfers between devices  1.92 us (3%)
  between operations  0.7 us (1%)
    all_to_all x1, blocking collectives, body(): lax.all_to_all(add_step(own, arrived), 'fsdp', 0, 0, tiled=True, axis_ind...  33.6 us
    all_to_all x1, blocking collectives, body(): lax.all_to_all(copies, 'dp', 0, 0, tiled=True, axis_index_groups=[dp_orde...  17.6 us
    pallas_call x1, Pallas kernels, outputs_step(): pl.pallas_call(outputs_kernel, in_specs=[whole] * 6, out_specs=[anywhere]...  2.05 us
    ppermute x1, starting transfers between devices, body(): lax.ppermute(pack_other(grouped, core), 'fsdp', [(i, i ^ 1) for i in rang...  1.92 us
    pallas_call x1, Pallas kernels, prepare(): pl.pallas_call(prepare_kernel, in_specs=[smem, smem, anywhere, whole], ou...  1.85 us
    pallas_call x1, Pallas kernels, pack_other(): pl.pallas_call(pack_kernel, in_specs=[smem, anywhere], out_specs=whole, o...  1.35 us
  transfers between devices with their start and end apart: 1, of which 1 were waited for; matrix products, arithmetic and copies ran while one was open for 0% of the time, Pallas kernels for 3%

profile of v7, /device:TPU:8, one launch (start us, length us, event | category | flops | bytes accessed | tf_op | source)
XLA Modules:
  0.0 60.0 jit_solution(17124912292489042468)
XLA Ops:
  0.6 0.0 copy-start
  0.7 1.4 %pack_other.1 = f32[8,224,128]{2,1,0:T(8,128)S(1)} custom-call(s32[1]{0:T(128)} %bitcast.core_ref, f32[2,224,8,128]{3,2,1,0:T(8,128)} %bitcast.11), custom_call_target="tpu_custom_call" | custom-call | bytes 1835008 | tf_op jit(solution)/shard_map/pack_other/pallas_call | solution.py:88
  2.0 1.9 %collective-permute-start = (f32[8,224,128]{2,1,0:T(8,128)S(1)}, f32[8,224,128]{2,1,0:T(8,128)S(1)}, u32[]{:S(2)}, u32[]{:S(2)}) collective-permute-start(f32[8,224,128]{2,1,0:T(8,128)S(1)} %pack_other.1), channel_id=1, source_target_pairs={{0,1},{1,0},{2,3},{3,2},{4,5},{5,4},{6,7},{7,6},{8,9},{9,8},{10,11... | collective-permute-start | bytes 2752520 | tf_op jit(solution)/shard_map/ppermute | solution.py:291
  3.9 0.0 copy-done
  4.0 1.9 %prepare.1 = (f32[8,224,128]{2,1,0:T(8,128)S(1)}, s32[4,128,224]{2,1,0:T(8,128)S(1)}, f32[8,224]{1,0:T(8,128)S(1)}, s32[128,224]{1,0:T(8,128)S(1)}) custom-call(s32[1]{0:T(128)} %bitcast.core_ref, s32[1]{0:T(128)} %bitcast.1.me_ref, f32[2,224,8,128]{3,2,1,0:T(8,128)} %bitcast.12, s32[32,4,448]{2,1,0:T(4,128)S(1)} %bitcast.9), custom_call_target="tpu_custom_call" | custom-call | flops 8257536 | bytes 1835008 | tf_op jit(solution)/shard_map/prepare/pallas_call | solution.py:142
  5.8 0.6 collective-permute-done.arrived_ref
  6.4 0.0 copy-start.2
  6.4 0.0 copy-start.3
  6.4 0.1 add_step.1
  6.5 0.0 copy-start.1
  6.5 33.6 %all_to_all.10.parts_ref = f32[8,224,128]{2,1,0:T(8,128)S(1)} all-to-all(f32[8,224,128]{2,1,0:T(8,128)S(1)} %add_step.1), channel_id=1, replica_groups={{14,12,10,8,6,4,2,0},{15,13,11,9,7,5,3,1},{30,28,26,24,22,20,18,16},{31..., dimensions={0} | all-to-all | bytes 1835008 | tf_op jit(solution)/shard_map/all_to_all | solution.py:295
  40.1 0.0 copy-done.2
  40.1 0.0 copy-done.3
  40.1 0.3 kept_step.1
  40.4 17.6 %all_to_all.11.kept_ref = f32[32,8,224]{2,1,0:T(8,128)S(1)} all-to-all(f32[32,8,224]{2,1,0:T(8,128)S(1)} %get-tuple-element.23), channel_id=1, replica_groups={{448,320,464,480,192,496,336,352,368,208,432,64,224,240,304,80,416,176,..., dimensions={0} | all-to-all | bytes 458752 | tf_op jit(solution)/shard_map/all_to_all | solution.py:297
  57.9 0.0 copy-done.1
  57.9 2.1 %outputs_step.1 = (f32[224,128]{1,0:T(8,128)}, f32[224,128]{1,0:T(8,128)}) custom-call(f32[32,8,224]{2,1,0:T(8,128)S(1)} %all_to_all.11.kept_ref, s32[4,128,224]{2,1,0:T(8,128)S(1)} %get-tuple-element.24.index_ref, f32[8,224]{1,0:T(8,128)S(1)} %get-tuple-element.25.own_ref, s32[128,224]{1,0:T(8,128)S(1)} %get-tuple-element.26.rows_ref, ...), custom_call_target="tpu_custom_call" | custom-call | flops 8257536 | bytes 458752 | tf_op jit(solution)/shard_map/outputs_step/pallas_call | solution.py:264
Async XLA Ops:
  0.6 3.3 %copy-start = (s32[32,1,4,448]{3,2,1,0:T(4,128)S(1)}, s32[32,1,4,448]{3,2,1,0:T(4,128)}, u32[]{:S(2)}) copy-start(s32[32,1,4,448]{3,2,1,0:T(4,128)} %param.7) | copy-start | bytes 688132
  2.0 4.4 %collective-permute-start = (f32[8,224,128]{2,1,0:T(8,128)S(1)}, f32[8,224,128]{2,1,0:T(8,128)S(1)}, u32[]{:S(2)}, u32[]{:S(2)}) collective-permute-start(f32[8,224,128]{2,1,0:T(8,128)S(1)} %pack_other.1), channel_id=1, source_target_pairs={{0,1},{1,0},{2,3},{3,2},{4,5},{5,4},{6,7},{7,6},{8,9},{9,8},{10,11... | collective-permute-start | bytes 2752520 | tf_op jit(solution)/shard_map/ppermute | solution.py:291
  6.4 33.7 %copy-start.2 = (bf16[256,256]{1,0:T(8,128)(2,1)S(1)}, bf16[256,256]{1,0:T(8,128)(2,1)}, u32[]{:S(2)}) copy-start(bf16[256,256]{1,0:T(8,128)(2,1)} %constant.26.clone.table_ref) | copy-start | bytes 393220
  6.4 33.7 %copy-start.3 = (f32[1,1,28672]{2,1,0:T(1,128)S(1)}, f32[1,1,28672]{2,1,0:T(1,128)}, u32[]{:S(2)}) copy-start(f32[1,1,28672]{2,1,0:T(1,128)} %param.6) | copy-start | bytes 344068
  6.5 51.4 %copy-start.1 = (bf16[256,256]{1,0:T(8,128)(2,1)S(1)}, bf16[256,256]{1,0:T(8,128)(2,1)}, u32[]{:S(2)}) copy-start(bf16[256,256]{1,0:T(8,128)(2,1)} %constant.27.clone.table_ref) | copy-start | bytes 393220

commit v8 on v7

--- a/solution.py
+++ b/solution.py
@@ -22,7 +22,8 @@
 
 
 def z_order(count):
-    return list(range(count - 1, -1, -1))
+    half = count // 2
+    return [z for pair in range(half - 1, -1, -1) for z in (pair + half, pair)]
 
 
 def dp_order():
@@ -97,7 +98,7 @@
     )(core, grouped)
 
 
-def prepare_kernel(core_ref, me_ref, grad_ref, places_ref, own_ref, index_ref, mine_ref, rows_ref, split, done):
+def prepare_kernel(core_ref, me_ref, grad_ref, places_ref, own_ref, index_ref, mine_ref, rows_ref, split, ordered, done):
     copies = row_copies(core_ref[0], grad_ref, own_ref, done)
     for copy in copies:
         copy.start()
@@ -112,7 +113,8 @@
         split[:, parity * count : (parity + 1) * count, :] = chosen.reshape(replicas, count, half)
     mine_ref[...] = split[me_ref[0]]
     level = lax.broadcasted_iota(jnp.int32, (block, half), 0).astype(f32)
-    order = dp_order()
+    for place, replica in enumerate(dp_order()):
+        ordered[place] = split[replica]
 
     def row_of(places, parity, shift):
         rows = jnp.full(level.shape, (count * (1 - parity)) << shift, jnp.int32)
@@ -124,12 +126,16 @@
     for parity in range(2):
         at = slice(parity * block, (parity + 1) * block)
         rows_ref[at, :] = row_of(lambda row: mine_ref[row : row + 1, :], parity, 0)
-        for word in range(replicas // 8):
+
+    @pl.loop(0, replicas // 8)
+    def _(word):
+        for parity in range(2):
             packed = jnp.zeros(level.shape, jnp.int32)
             for field in range(8):
-                replica = order[word * 8 + field]
-                packed = packed | row_of(lambda row: split[replica, row : row + 1, :], parity, 4 * field)
-            index_ref[word, at, :] = packed
+                place = word * 8 + field
+                packed = packed | row_of(lambda row: ordered[place, row : row + 1, :], parity, 4 * field)
+            index_ref[word, parity * block : (parity + 1) * block, :] = packed
+
     for copy in copies:
         copy.wait()
 
@@ -150,6 +156,7 @@
             jax.ShapeDtypeStruct((2 * block, half), jnp.int32),
         ],
         scratch_shapes=[
+            pltpu.VMEM((replicas, 2 * count, half), f32),
             pltpu.VMEM((replicas, 2 * count, half), f32),
             pltpu.SemaphoreType.DMA((rows,)),
         ],

time: 60.2 us -> 60.5 us (level)
  the two profiles are of different devices: /device:TPU:8 before, /device:TPU:72 now
where the time goes in v8:
time: 60.5 us; the launch traced here: 60.3 us
  blocking collectives  51.4 us (85%)
  Pallas kernels  5.46 us (9%)
  starting transfers between devices  1.92 us (3%)
  waiting for transfers between devices  0.77 us (1%)
  between operations  0.7 us (1%)
    all_to_all x1, blocking collectives, body(): lax.all_to_all(add_step(own, arrived), 'fsdp', 0, 0, tiled=True, axis_ind...  33.4 us
    all_to_all x1, blocking collectives, body(): lax.all_to_all(copies, 'dp', 0, 0, tiled=True, axis_index_groups=[dp_orde...  18 us
    pallas_call x1, Pallas kernels, outputs_step(): pl.pallas_call(outputs_kernel, in_specs=[whole] * 6, out_specs=[anywhere]...  2.05 us
    ppermute x1, starting transfers between devices, body(): lax.ppermute(pack_other(grouped, core), 'fsdp', [(i, i ^ 1) for i in rang...  1.92 us
    pallas_call x1, Pallas kernels, prepare(): pl.pallas_call(prepare_kernel, in_specs=[smem, smem, anywhere, whole], ou...  1.65 us
    pallas_call x1, Pallas kernels, pack_other(): pl.pallas_call(pack_kernel, in_specs=[smem, anywhere], out_specs=whole, o...  1.35 us
  transfers between devices with their start and end apart: 1, of which 1 were waited for; matrix products, arithmetic and copies ran while one was open for 0% of the time, Pallas kernels for 3%

profile of v8, /device:TPU:72, one launch (start us, length us, event | category | flops | bytes accessed | tf_op | source)
XLA Modules:
  0.0 60.3 jit_solution(12601214786963135780)
XLA Ops:
  0.6 0.0 copy-start
  0.7 1.4 %pack_other.1 = f32[8,224,128]{2,1,0:T(8,128)S(1)} custom-call(s32[1]{0:T(128)} %bitcast.core_ref, f32[2,224,8,128]{3,2,1,0:T(8,128)} %bitcast.11), custom_call_target="tpu_custom_call" | custom-call | bytes 1835008 | tf_op jit(solution)/shard_map/pack_other/pallas_call | solution.py:89
  2.0 1.9 %collective-permute-start = (f32[8,224,128]{2,1,0:T(8,128)S(1)}, f32[8,224,128]{2,1,0:T(8,128)S(1)}, u32[]{:S(2)}, u32[]{:S(2)}) collective-permute-start(f32[8,224,128]{2,1,0:T(8,128)S(1)} %pack_other.1), channel_id=1, source_target_pairs={{0,1},{1,0},{2,3},{3,2},{4,5},{5,4},{6,7},{7,6},{8,9},{9,8},{10,11... | collective-permute-start | bytes 2752520 | tf_op jit(solution)/shard_map/ppermute | solution.py:298
  3.9 0.0 copy-done
  4.0 1.6 %prepare.1 = (f32[8,224,128]{2,1,0:T(8,128)S(1)}, s32[4,128,224]{2,1,0:T(8,128)S(1)}, f32[8,224]{1,0:T(8,128)S(1)}, s32[128,224]{1,0:T(8,128)S(1)}) custom-call(s32[1]{0:T(128)} %bitcast.core_ref, s32[1]{0:T(128)} %bitcast.1.me_ref, f32[2,224,8,128]{3,2,1,0:T(8,128)} %bitcast.12, s32[32,4,448]{2,1,0:T(4,128)S(1)} %bitcast.9), custom_call_target="tpu_custom_call" | custom-call | flops 8257536 | bytes 1835008 | tf_op jit(solution)/shard_map/prepare/pallas_call | solution.py:148
  5.6 0.8 %collective-permute-done.arrived_ref = f32[8,224,128]{2,1,0:T(8,128)S(1)} collective-permute-done((f32[8,224,128]{2,1,0:T(8,128)S(1)}, f32[8,224,128]{2,1,0:T(8,128)S(1)}, u32[]{:S(2)}, u32[]{:S(2)}) %collective-permute-start) | collective-permute-done | bytes 917536 | tf_op jit(solution)/shard_map/ppermute | solution.py:298
  6.4 0.0 copy-start.2
  6.4 0.0 copy-start.3
  6.4 0.1 add_step.1
  6.5 0.0 copy-start.1
  6.5 33.4 %all_to_all.10.parts_ref = f32[8,224,128]{2,1,0:T(8,128)S(1)} all-to-all(f32[8,224,128]{2,1,0:T(8,128)S(1)} %add_step.1), channel_id=1, replica_groups={{14,6,12,4,10,2,8,0},{15,7,13,5,11,3,9,1},{30,22,28,20,26,18,24,16},{31..., dimensions={0} | all-to-all | bytes 1835008 | tf_op jit(solution)/shard_map/all_to_all | solution.py:302
  39.9 0.0 copy-done.2
  39.9 0.0 copy-done.3
  39.9 0.3 kept_step.1
  40.2 18.0 %all_to_all.11.kept_ref = f32[32,8,224]{2,1,0:T(8,128)S(1)} all-to-all(f32[32,8,224]{2,1,0:T(8,128)S(1)} %get-tuple-element.23), channel_id=1, replica_groups={{448,320,464,480,192,496,336,352,368,208,432,64,224,240,304,80,416,176,..., dimensions={0} | all-to-all | bytes 458752 | tf_op jit(solution)/shard_map/all_to_all | solution.py:304
  58.2 0.0 copy-done.1
  58.2 2.1 %outputs_step.1 = (f32[224,128]{1,0:T(8,128)}, f32[224,128]{1,0:T(8,128)}) custom-call(f32[32,8,224]{2,1,0:T(8,128)S(1)} %all_to_all.11.kept_ref, s32[4,128,224]{2,1,0:T(8,128)S(1)} %get-tuple-element.24.index_ref, f32[8,224]{1,0:T(8,128)S(1)} %get-tuple-element.25.own_ref, s32[128,224]{1,0:T(8,128)S(1)} %get-tuple-element.26.rows_ref, ...), custom_call_target="tpu_custom_call" | custom-call | flops 8257536 | bytes 458752 | tf_op jit(solution)/shard_map/outputs_step/pallas_call | solution.py:271
Async XLA Ops:
  0.6 3.3 %copy-start = (s32[32,1,4,448]{3,2,1,0:T(4,128)S(1)}, s32[32,1,4,448]{3,2,1,0:T(4,128)}, u32[]{:S(2)}) copy-start(s32[32,1,4,448]{3,2,1,0:T(4,128)} %param.7) | copy-start | bytes 688132
  2.0 4.4 %collective-permute-start = (f32[8,224,128]{2,1,0:T(8,128)S(1)}, f32[8,224,128]{2,1,0:T(8,128)S(1)}, u32[]{:S(2)}, u32[]{:S(2)}) collective-permute-start(f32[8,224,128]{2,1,0:T(8,128)S(1)} %pack_other.1), channel_id=1, source_target_pairs={{0,1},{1,0},{2,3},{3,2},{4,5},{5,4},{6,7},{7,6},{8,9},{9,8},{10,11... | collective-permute-start | bytes 2752520 | tf_op jit(solution)/shard_map/ppermute | solution.py:298
  6.4 33.5 %copy-start.2 = (bf16[256,256]{1,0:T(8,128)(2,1)S(1)}, bf16[256,256]{1,0:T(8,128)(2,1)}, u32[]{:S(2)}) copy-start(bf16[256,256]{1,0:T(8,128)(2,1)} %constant.26.clone.table_ref) | copy-start | bytes 393220
  6.4 33.5 %copy-start.3 = (f32[1,1,28672]{2,1,0:T(1,128)S(1)}, f32[1,1,28672]{2,1,0:T(1,128)}, u32[]{:S(2)}) copy-start(f32[1,1,28672]{2,1,0:T(1,128)} %param.6) | copy-start | bytes 344068
  6.5 51.7 %copy-start.1 = (bf16[256,256]{1,0:T(8,128)(2,1)S(1)}, bf16[256,256]{1,0:T(8,128)(2,1)}, u32[]{:S(2)}) copy-start(bf16[256,256]{1,0:T(8,128)(2,1)} %constant.27.clone.table_ref) | copy-start | bytes 393220

commit v9 on v8

--- a/solution.py
+++ b/solution.py
@@ -22,8 +22,7 @@
 
 
 def z_order(count):
-    half = count // 2
-    return [z for pair in range(half - 1, -1, -1) for z in (pair + half, pair)]
+    return list(range(count - 1, -1, -1))
 
 
 def dp_order():

time: 60.5 us -> 60.2 us (level)
  the two profiles are of different devices: /device:TPU:72 before, /device:TPU:8 now
where the time goes in v9:
time: 60.2 us; the launch traced here: 60 us
  blocking collectives  51.1 us (85%)
  Pallas kernels  5.46 us (9%)
  starting transfers between devices  1.92 us (3%)
  waiting for transfers between devices  0.77 us (1%)
  between operations  0.7 us (1%)
    all_to_all x1, blocking collectives, body(): lax.all_to_all(add_step(own, arrived), 'fsdp', 0, 0, tiled=True, axis_ind...  33.6 us
    all_to_all x1, blocking collectives, body(): lax.all_to_all(copies, 'dp', 0, 0, tiled=True, axis_index_groups=[dp_orde...  17.6 us
    pallas_call x1, Pallas kernels, outputs_step(): pl.pallas_call(outputs_kernel, in_specs=[whole] * 6, out_specs=[anywhere]...  2.05 us
    ppermute x1, starting transfers between devices, body(): lax.ppermute(pack_other(grouped, core), 'fsdp', [(i, i ^ 1) for i in rang...  1.92 us
    pallas_call x1, Pallas kernels, prepare(): pl.pallas_call(prepare_kernel, in_specs=[smem, smem, anywhere, whole], ou...  1.65 us
    pallas_call x1, Pallas kernels, pack_other(): pl.pallas_call(pack_kernel, in_specs=[smem, anywhere], out_specs=whole, o...  1.35 us
  transfers between devices with their start and end apart: 1, of which 1 were waited for; matrix products, arithmetic and copies ran while one was open for 0% of the time, Pallas kernels for 3%

profile of v9, /device:TPU:8, one launch (start us, length us, event | category | flops | bytes accessed | tf_op | source)
XLA Modules:
  0.0 60.0 jit_solution(7147096905820255585)
XLA Ops:
  0.6 0.0 copy-start
  0.7 1.4 %pack_other.1 = f32[8,224,128]{2,1,0:T(8,128)S(1)} custom-call(s32[1]{0:T(128)} %bitcast.core_ref, f32[2,224,8,128]{3,2,1,0:T(8,128)} %bitcast.11), custom_call_target="tpu_custom_call" | custom-call | bytes 1835008 | tf_op jit(solution)/shard_map/pack_other/pallas_call | solution.py:88
  2.0 1.9 %collective-permute-start = (f32[8,224,128]{2,1,0:T(8,128)S(1)}, f32[8,224,128]{2,1,0:T(8,128)S(1)}, u32[]{:S(2)}, u32[]{:S(2)}) collective-permute-start(f32[8,224,128]{2,1,0:T(8,128)S(1)} %pack_other.1), channel_id=1, source_target_pairs={{0,1},{1,0},{2,3},{3,2},{4,5},{5,4},{6,7},{7,6},{8,9},{9,8},{10,11... | collective-permute-start | bytes 2752520 | tf_op jit(solution)/shard_map/ppermute | solution.py:297
  3.9 0.0 copy-done
  4.0 1.6 %prepare.1 = (f32[8,224,128]{2,1,0:T(8,128)S(1)}, s32[4,128,224]{2,1,0:T(8,128)S(1)}, f32[8,224]{1,0:T(8,128)S(1)}, s32[128,224]{1,0:T(8,128)S(1)}) custom-call(s32[1]{0:T(128)} %bitcast.core_ref, s32[1]{0:T(128)} %bitcast.1.me_ref, f32[2,224,8,128]{3,2,1,0:T(8,128)} %bitcast.12, s32[32,4,448]{2,1,0:T(4,128)S(1)} %bitcast.9), custom_call_target="tpu_custom_call" | custom-call | flops 8257536 | bytes 1835008 | tf_op jit(solution)/shard_map/prepare/pallas_call | solution.py:147
  5.6 0.8 %collective-permute-done.arrived_ref = f32[8,224,128]{2,1,0:T(8,128)S(1)} collective-permute-done((f32[8,224,128]{2,1,0:T(8,128)S(1)}, f32[8,224,128]{2,1,0:T(8,128)S(1)}, u32[]{:S(2)}, u32[]{:S(2)}) %collective-permute-start) | collective-permute-done | bytes 917536 | tf_op jit(solution)/shard_map/ppermute | solution.py:297
  6.4 0.0 copy-start.2
  6.4 0.0 copy-start.3
  6.4 0.1 add_step.1
  6.5 0.0 copy-start.1
  6.5 33.6 %all_to_all.10.parts_ref = f32[8,224,128]{2,1,0:T(8,128)S(1)} all-to-all(f32[8,224,128]{2,1,0:T(8,128)S(1)} %add_step.1), channel_id=1, replica_groups={{14,12,10,8,6,4,2,0},{15,13,11,9,7,5,3,1},{30,28,26,24,22,20,18,16},{31..., dimensions={0} | all-to-all | bytes 1835008 | tf_op jit(solution)/shard_map/all_to_all | solution.py:301
  40.1 0.0 copy-done.2
  40.1 0.0 copy-done.3
  40.1 0.3 kept_step.1
  40.4 17.6 %all_to_all.11.kept_ref = f32[32,8,224]{2,1,0:T(8,128)S(1)} all-to-all(f32[32,8,224]{2,1,0:T(8,128)S(1)} %get-tuple-element.23), channel_id=1, replica_groups={{448,320,464,480,192,496,336,352,368,208,432,64,224,240,304,80,416,176,..., dimensions={0} | all-to-all | bytes 458752 | tf_op jit(solution)/shard_map/all_to_all | solution.py:303
  57.9 0.0 copy-done.1
  57.9 2.1 %outputs_step.1 = (f32[224,128]{1,0:T(8,128)}, f32[224,128]{1,0:T(8,128)}) custom-call(f32[32,8,224]{2,1,0:T(8,128)S(1)} %all_to_all.11.kept_ref, s32[4,128,224]{2,1,0:T(8,128)S(1)} %get-tuple-element.24.index_ref, f32[8,224]{1,0:T(8,128)S(1)} %get-tuple-element.25.own_ref, s32[128,224]{1,0:T(8,128)S(1)} %get-tuple-element.26.rows_ref, ...), custom_call_target="tpu_custom_call" | custom-call | flops 8257536 | bytes 458752 | tf_op jit(solution)/shard_map/outputs_step/pallas_call | solution.py:270
Async XLA Ops:
  0.6 3.3 %copy-start = (s32[32,1,4,448]{3,2,1,0:T(4,128)S(1)}, s32[32,1,4,448]{3,2,1,0:T(4,128)}, u32[]{:S(2)}) copy-start(s32[32,1,4,448]{3,2,1,0:T(4,128)} %param.7) | copy-start | bytes 688132
  2.0 4.4 %collective-permute-start = (f32[8,224,128]{2,1,0:T(8,128)S(1)}, f32[8,224,128]{2,1,0:T(8,128)S(1)}, u32[]{:S(2)}, u32[]{:S(2)}) collective-permute-start(f32[8,224,128]{2,1,0:T(8,128)S(1)} %pack_other.1), channel_id=1, source_target_pairs={{0,1},{1,0},{2,3},{3,2},{4,5},{5,4},{6,7},{7,6},{8,9},{9,8},{10,11... | collective-permute-start | bytes 2752520 | tf_op jit(solution)/shard_map/ppermute | solution.py:297
  6.4 33.7 %copy-start.2 = (bf16[256,256]{1,0:T(8,128)(2,1)S(1)}, bf16[256,256]{1,0:T(8,128)(2,1)}, u32[]{:S(2)}) copy-start(bf16[256,256]{1,0:T(8,128)(2,1)} %constant.26.clone.table_ref) | copy-start | bytes 393220
  6.4 33.7 %copy-start.3 = (f32[1,1,28672]{2,1,0:T(1,128)S(1)}, f32[1,1,28672]{2,1,0:T(1,128)}, u32[]{:S(2)}) copy-start(f32[1,1,28672]{2,1,0:T(1,128)} %param.6) | copy-start | bytes 344068
  6.5 51.4 %copy-start.1 = (bf16[256,256]{1,0:T(8,128)(2,1)S(1)}, bf16[256,256]{1,0:T(8,128)(2,1)}, u32[]{:S(2)}) copy-start(bf16[256,256]{1,0:T(8,128)(2,1)} %constant.27.clone.table_ref) | copy-start | bytes 393220

commit v10 on v9

--- a/solution.py
+++ b/solution.py
@@ -22,7 +22,7 @@
 
 
 def z_order(count):
-    return list(range(count - 1, -1, -1))
+    return list(range(count - 1, -1, -2)) + list(range(count - 2, -1, -2))
 
 
 def dp_order():

time: 60.2 us -> 60.5 us (level)
  the two profiles are of different devices: /device:TPU:8 before, /device:TPU:24 now
where the time goes in v10:
time: 60.5 us; the launch traced here: 60.3 us
  blocking collectives  51.4 us (85%)
  Pallas kernels  5.46 us (9%)
  starting transfers between devices  1.92 us (3%)
  waiting for transfers between devices  0.77 us (1%)
  between operations  0.7 us (1%)
    all_to_all x1, blocking collectives, body(): lax.all_to_all(add_step(own, arrived), 'fsdp', 0, 0, tiled=True, axis_ind...  34.9 us
    all_to_all x1, blocking collectives, body(): lax.all_to_all(copies, 'dp', 0, 0, tiled=True, axis_index_groups=[dp_orde...  16.6 us
    pallas_call x1, Pallas kernels, outputs_step(): pl.pallas_call(outputs_kernel, in_specs=[whole] * 6, out_specs=[anywhere]...  2.05 us
    ppermute x1, starting transfers between devices, body(): lax.ppermute(pack_other(grouped, core), 'fsdp', [(i, i ^ 1) for i in rang...  1.92 us
    pallas_call x1, Pallas kernels, prepare(): pl.pallas_call(prepare_kernel, in_specs=[smem, smem, anywhere, whole], ou...  1.64 us
    pallas_call x1, Pallas kernels, pack_other(): pl.pallas_call(pack_kernel, in_specs=[smem, anywhere], out_specs=whole, o...  1.35 us
  transfers between devices with their start and end apart: 1, of which 1 were waited for; matrix products, arithmetic and copies ran while one was open for 0% of the time, Pallas kernels for 3%

profile of v10, /device:TPU:24, one launch (start us, length us, event | category | flops | bytes accessed | tf_op | source)
XLA Modules:
  0.0 60.3 jit_solution(16789401808842298127)
XLA Ops:
  0.6 0.0 copy-start
  0.7 1.4 %pack_other.1 = f32[8,224,128]{2,1,0:T(8,128)S(1)} custom-call(s32[1]{0:T(128)} %bitcast.core_ref, f32[2,224,8,128]{3,2,1,0:T(8,128)} %bitcast.11), custom_call_target="tpu_custom_call" | custom-call | bytes 1835008 | tf_op jit(solution)/shard_map/pack_other/pallas_call | solution.py:88
  2.0 1.9 %collective-permute-start = (f32[8,224,128]{2,1,0:T(8,128)S(1)}, f32[8,224,128]{2,1,0:T(8,128)S(1)}, u32[]{:S(2)}, u32[]{:S(2)}) collective-permute-start(f32[8,224,128]{2,1,0:T(8,128)S(1)} %pack_other.1), channel_id=1, source_target_pairs={{0,1},{1,0},{2,3},{3,2},{4,5},{5,4},{6,7},{7,6},{8,9},{9,8},{10,11... | collective-permute-start | bytes 2752520 | tf_op jit(solution)/shard_map/ppermute | solution.py:297
  3.9 0.0 copy-done
  4.0 1.6 %prepare.1 = (f32[8,224,128]{2,1,0:T(8,128)S(1)}, s32[4,128,224]{2,1,0:T(8,128)S(1)}, f32[8,224]{1,0:T(8,128)S(1)}, s32[128,224]{1,0:T(8,128)S(1)}) custom-call(s32[1]{0:T(128)} %bitcast.core_ref, s32[1]{0:T(128)} %bitcast.1.me_ref, f32[2,224,8,128]{3,2,1,0:T(8,128)} %bitcast.12, s32[32,4,448]{2,1,0:T(4,128)S(1)} %bitcast.9), custom_call_target="tpu_custom_call" | custom-call | flops 8257536 | bytes 1835008 | tf_op jit(solution)/shard_map/prepare/pallas_call | solution.py:147
  5.6 0.8 %collective-permute-done.arrived_ref = f32[8,224,128]{2,1,0:T(8,128)S(1)} collective-permute-done((f32[8,224,128]{2,1,0:T(8,128)S(1)}, f32[8,224,128]{2,1,0:T(8,128)S(1)}, u32[]{:S(2)}, u32[]{:S(2)}) %collective-permute-start) | collective-permute-done | bytes 917536 | tf_op jit(solution)/shard_map/ppermute | solution.py:297
  6.4 0.0 copy-start.2
  6.4 0.0 copy-start.3
  6.4 0.1 add_step.1
  6.5 0.0 copy-start.1
  6.5 34.9 %all_to_all.10.parts_ref = f32[8,224,128]{2,1,0:T(8,128)S(1)} all-to-all(f32[8,224,128]{2,1,0:T(8,128)S(1)} %add_step.1), channel_id=1, replica_groups={{14,10,6,2,12,8,4,0},{15,11,7,3,13,9,5,1},{30,26,22,18,28,24,20,16},{31..., dimensions={0} | all-to-all | bytes 1835008 | tf_op jit(solution)/shard_map/all_to_all | solution.py:301
  41.4 0.0 copy-done.2
  41.4 0.0 copy-done.3
  41.4 0.3 kept_step.1
  41.7 16.6 %all_to_all.11.kept_ref = f32[32,8,224]{2,1,0:T(8,128)S(1)} all-to-all(f32[32,8,224]{2,1,0:T(8,128)S(1)} %get-tuple-element.23), channel_id=1, replica_groups={{448,320,464,480,192,496,336,352,368,208,432,64,224,240,304,80,416,176,..., dimensions={0} | all-to-all | bytes 458752 | tf_op jit(solution)/shard_map/all_to_all | solution.py:303
  58.2 0.0 copy-done.1
  58.2 2.1 %outputs_step.1 = (f32[224,128]{1,0:T(8,128)}, f32[224,128]{1,0:T(8,128)}) custom-call(f32[32,8,224]{2,1,0:T(8,128)S(1)} %all_to_all.11.kept_ref, s32[4,128,224]{2,1,0:T(8,128)S(1)} %get-tuple-element.24.index_ref, f32[8,224]{1,0:T(8,128)S(1)} %get-tuple-element.25.own_ref, s32[128,224]{1,0:T(8,128)S(1)} %get-tuple-element.26.rows_ref, ...), custom_call_target="tpu_custom_call" | custom-call | flops 8257536 | bytes 458752 | tf_op jit(solution)/shard_map/outputs_step/pallas_call | solution.py:270
Async XLA Ops:
  0.6 3.3 %copy-start = (s32[32,1,4,448]{3,2,1,0:T(4,128)S(1)}, s32[32,1,4,448]{3,2,1,0:T(4,128)}, u32[]{:S(2)}) copy-start(s32[32,1,4,448]{3,2,1,0:T(4,128)} %param.7) | copy-start | bytes 688132
  2.0 4.4 %collective-permute-start = (f32[8,224,128]{2,1,0:T(8,128)S(1)}, f32[8,224,128]{2,1,0:T(8,128)S(1)}, u32[]{:S(2)}, u32[]{:S(2)}) collective-permute-start(f32[8,224,128]{2,1,0:T(8,128)S(1)} %pack_other.1), channel_id=1, source_target_pairs={{0,1},{1,0},{2,3},{3,2},{4,5},{5,4},{6,7},{7,6},{8,9},{9,8},{10,11... | collective-permute-start | bytes 2752520 | tf_op jit(solution)/shard_map/ppermute | solution.py:297
  6.4 35.0 %copy-start.2 = (bf16[256,256]{1,0:T(8,128)(2,1)S(1)}, bf16[256,256]{1,0:T(8,128)(2,1)}, u32[]{:S(2)}) copy-start(bf16[256,256]{1,0:T(8,128)(2,1)} %constant.26.clone.table_ref) | copy-start | bytes 393220
  6.4 35.0 %copy-start.3 = (f32[1,1,28672]{2,1,0:T(1,128)S(1)}, f32[1,1,28672]{2,1,0:T(1,128)}, u32[]{:S(2)}) copy-start(f32[1,1,28672]{2,1,0:T(1,128)} %param.6) | copy-start | bytes 344068
  6.5 51.7 %copy-start.1 = (bf16[256,256]{1,0:T(8,128)(2,1)S(1)}, bf16[256,256]{1,0:T(8,128)(2,1)}, u32[]{:S(2)}) copy-start(bf16[256,256]{1,0:T(8,128)(2,1)} %constant.27.clone.table_ref) | copy-start | bytes 393220
